TPU v7x, 32 devices: a whole 2x2x4 slice. The times are simulated.
32 devices in a mesh: dp: 4 (over x, core), col: 8 (over z, y).
Axes of the slice: x: 2, y: 2, z: 4, core: 2. Of those that a mesh axis runs over, the one named last changes fastest.
Arguments:
- inputs: bfloat16 [32, 1024, 1024], P('dp', 'col'), may hold values from -6 to 6
- starts: int32 [32, 1024], P('dp', 'col'), may hold values from 0 to 1023, as said below
- cotangent: bfloat16 [32, 1024, 1024], P('dp', 'col'), may hold values from -6 to 6
- first_norm_gain: bfloat16 [1024], replicated, may hold values from 0.5 to 1.5
- shift_one: bfloat16 [1024], replicated, may hold values from -1.75 to 1.75
- w_qkv: bfloat16 [1024, 3072], replicated, may hold values from -0.1875 to 0.1875
- b_qkv: bfloat16 [3072], replicated, may hold values from -1.75 to 1.75
- w_out: bfloat16 [1024, 1024], replicated, may hold values from -1 to 1
- b_out: bfloat16 [1024], replicated, may hold values from -1.75 to 1.75
- second_norm_gain: bfloat16 [1024], replicated, may hold values from 0.5 to 1.5
- shift_two: bfloat16 [1024], replicated, may hold values from -1.75 to 1.75
- w_fc: bfloat16 [1024, 4096], replicated, may hold values from -0.1875 to 0.1875
- b_fc: bfloat16 [4096], replicated, may hold values from -1.75 to 1.75
- w_proj: bfloat16 [4096, 1024], replicated, may hold values from -0.09375 to 0.09375
- b_proj: bfloat16 [1024], replicated, may hold values from -1.75 to 1.75
- prefix_table: float32 [10, 512], replicated, may hold values from -6 to 6
- rep_w1: float32 [512, 512], replicated, may hold values from -0.25 to 0.25
- rep_b1: float32 [512], replicated, may hold values from -3 to 3
- rep_w2: float32 [512, 2048], P(None, 'col'), may hold values from -0.25 to 0.25
- rep_b2: float32 [2048], P('col'), may hold values from -3 to 3
Outputs:
- output: bfloat16 [32, 1024, 1024], P('dp', 'col')
- grad_input: bfloat16 [32, 1024, 1024], P('dp', 'col')
- grad_table: float32 [10, 512], replicated
- grad_w1: float32 [512, 512], replicated
- grad_b1: float32 [512], replicated
- grad_w2: float32 [512, 2048], P(None, 'col')
- grad_b2: float32 [2048], P('col')
Inputs may be any that keep to these rules, and one draw needn't show every extreme that they name: starts[r, q] is the first position of the document that holds token q of packed row r: it is equal over a document, equals q at a document's first token; position 0 begins a document, and position 1023 begins a document of one token in every packed row.
All inputs are finite; a program needn't handle non-finite values.
Results may differ from a plain program's by a relative error of at most 0.013.
Values may be sent and summed in bfloat16 or wider, within the bound.
A program may use at most 512 MiB of HBM per device.

v0:
```python
import jax
import jax.numpy as jnp
from jax import lax
from jax.sharding import PartitionSpec as P

H = 16


epsilon = 1e-05
gelu_coef = 0.7978845608028654
cubic_coef = 0.044715
group_heads = 4


def layer_normalize(values, norm_gain, norm_shift):
    center = values - jnp.mean(values, axis=-1, keepdims=True)
    inverse = lax.rsqrt(jnp.mean(center * center, axis=-1, keepdims=True) + epsilon)
    normed = center * inverse
    return (normed * norm_gain + norm_shift, normed, inverse)


def norm_backward_pass(gradient, norm_gain, normed, inverse):
    scaled = gradient * norm_gain
    centered = scaled - jnp.mean(scaled, axis=-1, keepdims=True)
    return inverse * (centered - normed * jnp.mean(scaled * normed, axis=-1, keepdims=True))


def gelu_parts(upper_rows):
    tangent = jnp.tanh(gelu_coef * (upper_rows + cubic_coef * upper_rows * upper_rows * upper_rows))
    gelu_value = 0.5 * upper_rows * (1.0 + tangent)
    gelu_slope = 0.5 * (1.0 + tangent) + 0.5 * upper_rows * (
        1.0 - tangent * tangent
    ) * gelu_coef * (1.0 + 3.0 * cubic_coef * upper_rows * upper_rows)
    return (gelu_value, gelu_slope)


def dense_product(pattern, left_side, right_side):
    return jnp.einsum(pattern, left_side, right_side, preferred_element_type=jnp.float32)


def score_pair(queries, key_heads, prefix_keys, allowed, score_scale):
    token_scores = dense_product("rqhe,rkhe->rhqk", queries, key_heads) * score_scale
    token_scores = jnp.where(allowed[:, None], token_scores, -jnp.inf)
    prefix_scores = dense_product("rqhe,phe->rhqp", queries, prefix_keys) * score_scale
    return (token_scores, prefix_scores)


def forward_group(queries, key_heads, values, prefix_keys, prefix_values, allowed, score_scale):
    token_scores, prefix_scores = score_pair(queries, key_heads, prefix_keys, allowed, score_scale)
    row_peak = jnp.maximum(jnp.max(token_scores, axis=-1), jnp.max(prefix_scores, axis=-1))
    exp_total = jnp.sum(jnp.exp(token_scores - row_peak[..., None]), axis=-1) + jnp.sum(
        jnp.exp(prefix_scores - row_peak[..., None]), axis=-1
    )
    logsum = row_peak + jnp.log(exp_total)
    token_weights = jnp.exp(token_scores - logsum[..., None]).astype(jnp.bfloat16)
    prefix_weights = jnp.exp(prefix_scores - logsum[..., None]).astype(jnp.bfloat16)
    attended = dense_product("rhqk,rkhe->rqhe", token_weights, values) + dense_product(
        "rhqp,phe->rqhe", prefix_weights, prefix_values
    )
    return (attended, logsum)


def query_side(
    queries, key_heads, values, prefix_keys, prefix_values, grad_out, logsum, allowed, score_scale
):
    token_scores, prefix_scores = score_pair(queries, key_heads, prefix_keys, allowed, score_scale)
    token_weights = jnp.exp(token_scores - logsum[..., None])
    prefix_weights = jnp.exp(prefix_scores - logsum[..., None])
    token_dprobs = dense_product("rqhe,rkhe->rhqk", grad_out, values)
    prefix_dprobs = dense_product("rqhe,phe->rhqp", grad_out, prefix_values)
    dot_delta = jnp.sum(token_dprobs * token_weights, axis=-1) + jnp.sum(
        prefix_dprobs * prefix_weights, axis=-1
    )
    token_dscores = (token_weights * (token_dprobs - dot_delta[..., None])).astype(jnp.bfloat16)
    prefix_dscores = (prefix_weights * (prefix_dprobs - dot_delta[..., None])).astype(jnp.bfloat16)
    grad_queries = (
        dense_product("rhqk,rkhe->rqhe", token_dscores, key_heads)
        + dense_product("rhqp,phe->rqhe", prefix_dscores, prefix_keys)
    ) * score_scale
    grad_pkeys = dense_product("rhqp,rqhe->phe", prefix_dscores, queries) * score_scale
    grad_pvalues = dense_product("rhqp,rqhe->phe", prefix_weights.astype(jnp.bfloat16), grad_out)
    return (grad_queries, grad_pkeys, grad_pvalues, token_weights, token_dscores, dot_delta)


def on_device(
    inputs,
    starts,
    cotangent,
    first_norm_gain,
    shift_one,
    w_qkv,
    b_qkv,
    w_out,
    b_out,
    second_norm_gain,
    shift_two,
    w_fc,
    b_fc,
    w_proj,
    b_proj,
    prefix_table,
    rep_w1,
    rep_b1,
    rep_w2,
    rep_b2,
):
    low_type = jnp.bfloat16
    complete_dtype_kind = jnp.float32
    col_count = lax.axis_size("col")
    row_count, piece_len, model_width = inputs.shape
    length = piece_len * col_count
    head_size = model_width // H
    group_size = min(group_heads, H)
    group_count = H // group_size
    score_scale = head_size ** (-0.5)
    position_first = lax.axis_index("col") * piece_len
    pre_act = (
        dense_product("pd,dh->ph", prefix_table.astype(low_type), rep_w1.astype(low_type)) + rep_b1
    )
    hidden = jnp.tanh(pre_act)
    hidden_low = hidden.astype(low_type)
    w2_low = rep_w2.astype(low_type)
    own_cols = (dense_product("ph,hc->pc", hidden_low, w2_low) + rep_b2).astype(low_type)
    prefix_all = lax.all_gather(own_cols, "col", axis=1, tiled=True)
    prefix_keys = prefix_all[:, :model_width].reshape(-1, H, head_size)
    prefix_values = prefix_all[:, model_width:].reshape(-1, H, head_size)
    residual = inputs.astype(complete_dtype_kind)
    first_normed_rows, first_standardized, first_inverse_deviation = layer_normalize(
        residual, first_norm_gain.astype(complete_dtype_kind), shift_one.astype(complete_dtype_kind)
    )
    mixed_rows = dense_product(
        "rpd,de->rpe", first_normed_rows.astype(low_type), w_qkv
    ) + b_qkv.astype(complete_dtype_kind)
    queries = mixed_rows[..., :model_width].astype(low_type)
    key_rows = mixed_rows[..., model_width : 2 * model_width].astype(low_type)
    value_rows = mixed_rows[..., 2 * model_width :].astype(low_type)
    keys_whole, values_whole = (
        lax.all_gather(key_rows, "col", axis=1, tiled=True),
        lax.all_gather(value_rows, "col", axis=1, tiled=True),
    )
    query_heads = queries.reshape(row_count, piece_len, H, head_size)
    key_heads = keys_whole.reshape(row_count, length, H, head_size)
    value_heads = values_whole.reshape(row_count, length, H, head_size)
    query_pos = position_first + jnp.arange(piece_len, dtype=jnp.int32)
    key_pos = jnp.arange(length, dtype=jnp.int32)
    allowed = (key_pos[None, None, :] >= starts[:, :, None]) & (
        key_pos[None, None, :] <= query_pos[None, :, None]
    )

    def forward_step(group_index, state_pair):
        attended_all, logsum_all = state_pair
        head_first = group_index * group_size
        attended, logsum = forward_group(
            lax.dynamic_slice_in_dim(query_heads, head_first, group_size, 2),
            lax.dynamic_slice_in_dim(key_heads, head_first, group_size, 2),
            lax.dynamic_slice_in_dim(value_heads, head_first, group_size, 2),
            lax.dynamic_slice_in_dim(prefix_keys, head_first, group_size, 1),
            lax.dynamic_slice_in_dim(prefix_values, head_first, group_size, 1),
            allowed,
            score_scale,
        )
        return (
            lax.dynamic_update_slice_in_dim(attended_all, attended, head_first, 2),
            lax.dynamic_update_slice_in_dim(logsum_all, logsum, head_first, 1),
        )

    attended_all, logsum_all = lax.fori_loop(
        0,
        group_count,
        forward_step,
        (
            jnp.zeros((row_count, piece_len, H, head_size), complete_dtype_kind),
            jnp.zeros((row_count, H, piece_len), complete_dtype_kind),
        ),
    )
    attended_low = attended_all.reshape(row_count, piece_len, model_width).astype(low_type)
    middle = (
        residual
        + dense_product("rpd,de->rpe", attended_low, w_out)
        + b_out.astype(complete_dtype_kind)
    )
    second_normed_rows, second_standardized, second_inverse_deviation = layer_normalize(
        middle, second_norm_gain.astype(complete_dtype_kind), shift_two.astype(complete_dtype_kind)
    )
    upper_rows = dense_product(
        "rpd,df->rpf", second_normed_rows.astype(low_type), w_fc
    ) + b_fc.astype(complete_dtype_kind)
    activation, gelu_slope = gelu_parts(upper_rows)
    result = (
        middle
        + dense_product("rpf,fd->rpd", activation.astype(low_type), w_proj)
        + b_proj.astype(complete_dtype_kind)
    )
    output = result.astype(low_type)
    grad_act = dense_product("rpd,fd->rpf", cotangent, w_proj)
    grad_upper = (grad_act * gelu_slope).astype(low_type)
    gradient_second_normed = dense_product("rpf,df->rpd", grad_upper, w_fc)
    gradient_midpoint = cotangent.astype(complete_dtype_kind) + norm_backward_pass(
        gradient_second_normed,
        second_norm_gain.astype(complete_dtype_kind),
        second_standardized,
        second_inverse_deviation,
    )
    grad_attended = dense_product("rpe,de->rpd", gradient_midpoint.astype(low_type), w_out).astype(
        low_type
    )
    grad_heads = grad_attended.reshape(row_count, piece_len, H, head_size)

    def group_inputs(head_first):
        return (
            lax.dynamic_slice_in_dim(query_heads, head_first, group_size, 2),
            lax.dynamic_slice_in_dim(key_heads, head_first, group_size, 2),
            lax.dynamic_slice_in_dim(value_heads, head_first, group_size, 2),
            lax.dynamic_slice_in_dim(prefix_keys, head_first, group_size, 1),
            lax.dynamic_slice_in_dim(prefix_values, head_first, group_size, 1),
            lax.dynamic_slice_in_dim(grad_heads, head_first, group_size, 2),
            lax.dynamic_slice_in_dim(logsum_all, head_first, group_size, 1),
        )

    prefix_zero = jnp.zeros((prefix_keys.shape[0], H, head_size), complete_dtype_kind)
    query_zero = jnp.zeros((row_count, piece_len, H, head_size), complete_dtype_kind)

    def back_step(group_index, state_all):
        grad_q_all, grad_k_all, grad_v_all, grad_pk_all, grad_pv_all = state_all
        head_first = group_index * group_size
        group_q, group_k, group_v, group_pk, group_pv, group_out, group_logsum = group_inputs(
            head_first
        )
        grad_q, grad_pk, grad_pv, token_weights, token_dscores, dot_delta = query_side(
            group_q,
            group_k,
            group_v,
            group_pk,
            group_pv,
            group_out,
            group_logsum,
            allowed,
            score_scale,
        )
        grad_k = dense_product("rhqk,rqhe->rkhe", token_dscores, group_q) * score_scale
        grad_v = dense_product("rhqk,rqhe->rkhe", token_weights.astype(low_type), group_out)
        return (
            lax.dynamic_update_slice_in_dim(grad_q_all, grad_q, head_first, 2),
            lax.dynamic_update_slice_in_dim(grad_k_all, grad_k, head_first, 2),
            lax.dynamic_update_slice_in_dim(grad_v_all, grad_v, head_first, 2),
            lax.dynamic_update_slice_in_dim(grad_pk_all, grad_pk, head_first, 1),
            lax.dynamic_update_slice_in_dim(grad_pv_all, grad_pv, head_first, 1),
        )

    key_zero = jnp.zeros((row_count, length, H, head_size), complete_dtype_kind)
    grad_q_all, grad_k_all, grad_v_all, grad_pk_all, grad_pv_all = lax.fori_loop(
        0, group_count, back_step, (query_zero, key_zero, key_zero, prefix_zero, prefix_zero)
    )
    key_terms = grad_k_all.reshape(row_count, length, model_width)
    value_terms = grad_v_all.reshape(row_count, length, model_width)
    key_grad, value_grad = (
        lax.psum_scatter(key_terms, "col", scatter_dimension=1, tiled=True),
        lax.psum_scatter(value_terms, "col", scatter_dimension=1, tiled=True),
    )
    grad_mixed = jnp.concatenate(
        [
            grad_q_all.reshape(row_count, piece_len, model_width).astype(low_type),
            key_grad.astype(low_type),
            value_grad.astype(low_type),
        ],
        axis=-1,
    )
    gradient_first_normed = dense_product("rpe,de->rpd", grad_mixed, w_qkv)
    grad_input = (
        gradient_midpoint
        + norm_backward_pass(
            gradient_first_normed,
            first_norm_gain.astype(complete_dtype_kind),
            first_standardized,
            first_inverse_deviation,
        )
    ).astype(low_type)
    prefix_rows = prefix_keys.shape[0]
    prefix_local = jnp.concatenate(
        [
            grad_pk_all.reshape(prefix_rows, model_width),
            grad_pv_all.reshape(prefix_rows, model_width),
        ],
        axis=1,
    )
    own_grad = lax.psum_scatter(prefix_local, "col", scatter_dimension=1, tiled=True)
    own_grad = lax.psum(own_grad, "dp")
    own_low = own_grad.astype(low_type)
    grad_w2 = dense_product("ph,pc->hc", hidden_low, own_low)
    grad_b2 = jnp.sum(own_low.astype(complete_dtype_kind), axis=0)
    hidden_part = dense_product("pc,hc->ph", own_low, w2_low)
    grad_hidden = lax.psum(hidden_part, "col")
    grad_pre = (grad_hidden * (1.0 - hidden * hidden)).astype(low_type)
    grad_w1 = dense_product("pd,ph->dh", prefix_table.astype(low_type), grad_pre)
    grad_b1 = jnp.sum(grad_pre.astype(complete_dtype_kind), axis=0)
    grad_table = dense_product("ph,dh->pd", grad_pre, rep_w1.astype(low_type))
    return (output, grad_input, grad_table, grad_w1, grad_b1, grad_w2, grad_b2)


def solution(mesh):
    return jax.shard_map(
        on_device,
        mesh=mesh,
        in_specs=(
            P("dp", "col", None),
            P("dp", "col"),
            P("dp", "col", None),
            P(),
            P(),
            P(),
            P(),
            P(),
            P(),
            P(),
            P(),
            P(),
            P(),
            P(),
            P(),
            P(),
            P(),
            P(),
            P(None, "col"),
            P("col"),
        ),
        out_specs=(
            P("dp", "col", None),
            P("dp", "col", None),
            P(),
            P(),
            P(),
            P(None, "col"),
            P("col"),
        ),
        check_vma=False,
    )
```

profile of v0, /device:TPU:0, one launch (start us, length us, event | category | flops | bytes accessed | tf_op | source)
XLA Modules:
  0.0 2158.9 jit_solution(11164334197813312186)
XLA Ops:
  31.9 33.0 %all_gather.11 = bf16[10,2048]{1,0:T(8,128)(2,1)S(1)} all-gather(bf16[10,256]{1,0:T(8,128)(2,1)S(1)} %fusion.139), channel_id=1, replica_groups=mesh['dp'=4,'col'=8] {'col'}, dimensions={1}, use_global_device_ids=true | all-gather | bytes 46080 | tf_op jit(solution)/shard_map/all_gather | solution.py:124
  70.4 187.0 %all-gather.5.cloned.1.call-done = bf16[8,1024,1024]{2,1,0:T(8,128)(2,1)} async-done(((bf16[8,128,1024]{2,1,0:T(8,128)(2,1)}), bf16[8,1024,1024]{2,1,0:T(8,128)(2,1)}) %all-gather.5.cloned.1.call-update) | async-done | bytes 16777232 | tf_op jit(solution)/shard_map/all_gather | solution.py:138
  257.5 22.0 %copy.152 = bf16[8,1024,1024]{1,2,0:T(8,128)(2,1)} copy(bf16[8,1024,1024]{2,1,0:T(8,128)(2,1)} %all-gather.5.cloned.1.call-done) | data formatting | bytes 33554432 | tf_op jit(solution)/shard_map/all_gather | solution.py:138
  279.4 206.0 %all-gather.3.cloned.1.call-done = bf16[8,1024,1024]{2,1,0:T(8,128)(2,1)} async-done(((bf16[8,128,1024]{2,1,0:T(8,128)(2,1)}), bf16[8,1024,1024]{2,1,0:T(8,128)(2,1)}) %all-gather.3.cloned.1.call-update) | async-done | bytes 16777232 | tf_op jit(solution)/shard_map/all_gather | solution.py:139
  485.4 21.5 copy.150
  509.5 120.8 %while.38 = (s32[]{:T(128)}, bf16[8,128,16,64]{1,3,2,0:T(8,128)(2,1)}, f32[8,16,128]{2,0,1:T(8,128)}, bf16[8,1024,16,64]{1,3,2,0:T(8,128)(2,1)}, bf16[8,128,16,6...) while((s32[]{:T(128)}, ...), condition=%wide.region_7.8_spmd.clone, body=%wide.region_2.7_spmd.clone.sunk | while | flops 1132965888 | bytes 135208160 | solution.py:167
  524.8 12.4 fusion.222
  554.9 12.4 fusion.222
  585.0 12.4 fusion.222
  615.1 12.4 fusion.222
  649.6 31.2 %multiply_reduce_fusion.5 = (f32[8,128]{1,0:T(8,128)S(1)}, f32[8,128]{1,0:T(8,128)S(1)}, f32[8,128,1024]{2,1,0:T(8,128)}) fusion(f32[1024]{0:T(1024)S(1)} %copy-done.28, f32[8,128]{1,0:T(8,128)S(1)} %add_rsqrt_fusion, f32[8,128,1024]{2,1,0:T(8,128)} %copy-done.4, f32[8,128]{1,0:T(8,128)S(1)} %broadcast_multiply_fusion.4, bf16[1024,4096]{1,0:T(8,128)(2,1)} %param.35, ...), kind=kOutput, calls=%fused_computation.148 | convolution fusion | flops 17270046720 | bytes 44077056 | tf_op jit(solution)/shard_map/rpf,df->rpd/dot_general | solution.py:38
  717.3 259.8 %while.39 = (s32[]{:T(128)}, bf16[8,128,16,64]{1,3,2,0:T(8,128)(2,1)}, f32[8,1024,16,64]{1,3,2,0:T(8,128)}, f32[8,1024,16,64]{1,3,2,0:T(8,128)}, f32[10,16,64]{2...) while((s32[]{:T(128)}, ...), condition=%wide.region_15.16_spmd.clone, body=%wide.region_12.15_spmd.clone.sunk | while | flops 2753362432 | bytes 192729424 | solution.py:251
  733.1 15.2 multiply_reduce_fusion.8
  798.1 15.2 multiply_reduce_fusion.8
  863.0 15.2 multiply_reduce_fusion.8
  927.8 15.2 multiply_reduce_fusion.8
  978.1 32.2 %copy.160 = f32[8,1024,1024]{2,1,0:T(8,128)} copy(f32[8,1024,1024]{1,2,0:T(8,128)} %bitcast.178) | data formatting | bytes 67108864 | tf_op jit(solution)/shard_map/reshape | solution.py:254
  1010.4 32.0 %copy.161 = f32[8,1024,1024]{2,1,0:T(8,128)} copy(f32[8,1024,1024]{1,2,0:T(8,128)} %bitcast.177) | data formatting | bytes 67108864 | tf_op jit(solution)/shard_map/reshape | solution.py:255
  1046.6 18.9 add_convert_fusion.1
  1065.5 12.1 psum.14
  1077.7 37.2 %psum.15 = f32[10,512]{1,0:T(8,128)S(1)} all-reduce(f32[10,512]{1,0:T(8,128)S(1)} %fusion.143), channel_id=1, replica_groups=mesh['dp'=4,'col'=8] {'col'}, use_global_device_ids=true, to_apply=%region_22.23 | all-reduce | flops 5120 | bytes 40960 | tf_op jit(solution)/shard_map/psum | solution.py:292
  1119.7 464.3 %reduce-scatter.4.cloned.1.call-done = f32[8,128,1024]{2,1,0:T(8,128)} async-done(((f32[8,1024,1024]{2,1,0:T(8,128)}), f32[8,128,1024]{2,1,0:T(8,128)}) %reduce-scatter.4.cloned.1.call-update) | async-done | bytes 4194320 | tf_op jit(solution)/shard_map/reduce_scatter | solution.py:257
  1587.9 541.7 %reduce-scatter.6.cloned.1.call-done = f32[8,128,1024]{2,1,0:T(8,128)} async-done(((f32[8,1024,1024]{2,1,0:T(8,128)}), f32[8,128,1024]{2,1,0:T(8,128)}) %reduce-scatter.6.cloned.1.call-update) | async-done | bytes 4194320 | tf_op jit(solution)/shard_map/reduce_scatter | solution.py:258
  2133.5 12.5 multiply_reduce_fusion.4
  (301 shorter events, 381.2 us)
Async XLA Ops:
  7.2 623.1 %copy-start = (bf16[1024,1024]{1,0:T(8,128)(2,1)S(1)}, bf16[1024,1024]{1,0:T(8,128)(2,1)}, u32[]{:S(2)}) copy-start(bf16[1024,1024]{1,0:T(8,128)(2,1)} %param.31) | copy-start | bytes 6291460
  7.2 250.3 %all-gather.5.cloned.1.call-start = ((), (), s32[]{:S(2)}) async-start(), calls=%async_computation.4 | async-start | bytes 18874368 | tf_op jit(solution)/shard_map/all_gather | solution.py:138
  26.7 458.8 %all-gather.3.cloned.1.call-start = ((), (), s32[]{:S(2)}) async-start(), calls=%async_computation.3 | async-start | bytes 18874368 | tf_op jit(solution)/shard_map/all_gather | solution.py:139
  27.4 1038.1 %reduce-scatter.8.cloned.1.call-start = ((), (), s32[]{:S(2)}) async-start(), calls=%async_computation.7 | async-start | bytes 147456 | tf_op jit(solution)/shard_map/reduce_scatter | solution.py:286
  635.5 45.2 %copy-start.22 = (f32[8,128]{1,0:T(8,128)}, f32[8,128]{1,0:T(8,128)S(1)}, u32[]{:S(2)}) copy-start(f32[8,128]{1,0:T(8,128)S(1)} %broadcast_multiply_fusion.4) | copy-start | bytes 12292
  637.5 43.3 %copy-start.30 = (f32[8,128]{1,0:T(8,128)}, f32[8,128]{1,0:T(8,128)S(1)}, u32[]{:S(2)}) copy-start(f32[8,128]{1,0:T(8,128)S(1)} %add_rsqrt_fusion) | copy-start | bytes 12292
  978.0 606.0 %reduce-scatter.4.cloned.1.call-start = ((), (), s32[]{:S(2)}) async-start(), calls=%async_computation.5 | async-start | bytes 37748736 | tf_op jit(solution)/shard_map/reduce_scatter | solution.py:257
  1010.3 1119.3 %reduce-scatter.6.cloned.1.call-start = ((), (), s32[]{:S(2)}) async-start(), calls=%async_computation.6 | async-start | bytes 37748736 | tf_op jit(solution)/shard_map/reduce_scatter | solution.py:258
  1046.6 31.0 %copy-start.15 = (f32[512,256]{1,0:T(8,128)S(1)}, f32[512,256]{1,0:T(8,128)}, u32[]{:S(2)}) copy-start(f32[512,256]{1,0:T(8,128)} %param.42) | copy-start | bytes 1572868
  1046.6 68.4 %copy-start.17 = (f32[10,512]{1,0:T(8,128)S(1)}, f32[10,512]{1,0:T(8,128)}, u32[]{:S(2)}) copy-start(f32[10,512]{1,0:T(8,128)} %copy-done.16) | copy-start | bytes 61444
  1046.6 69.0 %copy-start.19 = (f32[10,512]{1,0:T(8,128)S(1)}, f32[10,512]{1,0:T(8,128)}, u32[]{:S(2)}) copy-start(f32[10,512]{1,0:T(8,128)} %param.39) | copy-start | bytes 61444
  1065.5 53.4 %copy-start.13 = (f32[512,512]{1,0:T(8,128)S(1)}, f32[512,512]{1,0:T(8,128)}, u32[]{:S(2)}) copy-start(f32[512,512]{1,0:T(8,128)} %param.40) | copy-start | bytes 3145732
  1587.9 545.6 %copy-start.7 = (bf16[8,128,1024]{2,1,0:T(8,128)(2,1)S(1)}, bf16[8,128,1024]{2,1,0:T(8,128)(2,1)}, u32[]{:S(2)}) copy-start(bf16[8,128,1024]{2,1,0:T(8,128)(2,1)} %param.24) | copy-start | bytes 6291460
  1587.9 545.6 %copy-start.21 = (f32[8,128]{1,0:T(8,128)S(1)}, f32[8,128]{1,0:T(8,128)}, u32[]{:S(2)}) copy-start(f32[8,128]{1,0:T(8,128)} %copy-done.20) | copy-start | bytes 12292
  1587.9 545.6 %copy-start.25 = (f32[1024]{0:T(1024)S(1)}, f32[1024]{0:T(1024)}, u32[]{:S(2)}) copy-start(f32[1024]{0:T(1024)} %copy-done.24) | copy-start | bytes 12292
  1587.9 545.6 %copy-start.27 = (f32[8,128]{1,0:T(8,128)S(1)}, f32[8,128]{1,0:T(8,128)}, u32[]{:S(2)}) copy-start(f32[8,128]{1,0:T(8,128)} %copy-done.26) | copy-start | bytes 12292
  2133.4 12.6 copy-start.5
  2133.4 12.6 copy-start.8
  2133.5 12.6 copy-start.14
  2133.5 12.6 copy-start.23
  2133.5 12.6 copy-start.29
  2133.5 12.6 copy-start.31
  2133.5 12.6 copy-start.33
  2133.5 12.6 copy-start.35
  (42 other events, 231.6 us)
Sparse Core Ops, SparseCore 0:
  26.8 230.6 all-gather.4
  259.6 225.7 all-gather.2
  978.1 59.4 reduce-scatter.7
  1041.3 542.7 reduce-scatter.3
  1587.6 541.8 reduce-scatter.5
where the time goes:
time: 2170 us; the launch traced here: 2160 us
  waiting for transfers between devices  1400 us (65%)
  matrix products  388 us (18%)
  local copies, waits for them, and re-layouts  170 us (8%)
  other arithmetic  102 us (5%)
  blocking collectives  82.3 us (4%)
    reduce_scatter x1, waiting for transfers between devices, on_device(): lax.psum_scatter(value_terms, 'col', scatter_dimension=1, tiled=True)  542 us
    reduce_scatter x1, waiting for transfers between devices, on_device(): lax.psum_scatter(key_terms, 'col', scatter_dimension=1, tiled=True)  464 us
    dot_general x69, matrix products, dense_product(): jnp.einsum(pattern, left_side, right_side, preferred_element_type=jnp.flo...  388 us
    all_gather x1, waiting for transfers between devices, on_device(): lax.all_gather(value_rows, 'col', axis=1, tiled=True)  206 us
    all_gather x1, waiting for transfers between devices, on_device(): lax.all_gather(key_rows, 'col', axis=1, tiled=True)  187 us
    convert_element_type x4, other arithmetic, query_side(): (token_weights * (token_dprobs - dot_delta[..., None])).astype(jnp.bfloat16)  45.3 us
  transfers between devices with their start and end apart: 5, of which 4 were waited for; matrix products, arithmetic and copies ran while one was open for 6% of the time, Pallas kernels for 0%

commit v1 on v0

v1 whole, which is shorter than its diff:
```python
import functools

import jax
import jax.numpy as jnp
from jax import lax
from jax.experimental import pallas as pl
from jax.experimental.pallas import tpu as pltpu
from jax.sharding import PartitionSpec as P

H = 16
HEAD = 64
PAIR = 2 * HEAD
BLOCK = 256
PRE = 16

epsilon = 1e-05
gelu_coef = 0.7978845608028654
cubic_coef = 0.044715
low_type = jnp.bfloat16
wide = jnp.float32
NT = (((1,), (1,)), ((), ()))


def layer_normalize(values, norm_gain, norm_shift):
    center = values - jnp.mean(values, axis=-1, keepdims=True)
    inverse = lax.rsqrt(jnp.mean(center * center, axis=-1, keepdims=True) + epsilon)
    normed = center * inverse
    return (normed * norm_gain + norm_shift, normed, inverse)


def norm_backward_pass(gradient, norm_gain, normed, inverse):
    scaled = gradient * norm_gain
    centered = scaled - jnp.mean(scaled, axis=-1, keepdims=True)
    return inverse * (centered - normed * jnp.mean(scaled * normed, axis=-1, keepdims=True))


def gelu_parts(upper_rows):
    tangent = jnp.tanh(gelu_coef * (upper_rows + cubic_coef * upper_rows * upper_rows * upper_rows))
    gelu_value = 0.5 * upper_rows * (1.0 + tangent)
    gelu_slope = 0.5 * (1.0 + tangent) + 0.5 * upper_rows * (
        1.0 - tangent * tangent
    ) * gelu_coef * (1.0 + 3.0 * cubic_coef * upper_rows * upper_rows)
    return (gelu_value, gelu_slope)


def dense_product(pattern, left_side, right_side):
    return jnp.einsum(pattern, left_side, right_side, preferred_element_type=jnp.float32)


def dot_nt(a, b):
    return lax.dot_general(a, b, NT, preferred_element_type=wide)


def dot(a, b):
    return jnp.dot(a, b, preferred_element_type=wide)


def head_mask(values, which):
    lane = lax.broadcasted_iota(jnp.int32, values.shape, 1)
    keep = (lane < HEAD) if which == 0 else (lane >= HEAD)
    return jnp.where(keep, values, jnp.zeros_like(values))


def token_mask(scores, start, block_q, block_k):
    key = block_k * BLOCK + lax.broadcasted_iota(jnp.int32, scores.shape, 0)
    keep = key >= start
    if block_q == block_k:
        query = block_q * BLOCK + lax.broadcasted_iota(jnp.int32, scores.shape, 1)
        keep = keep & (key <= query)
    return jnp.where(keep, scores, -jnp.inf)


def prefix_mask(scores, count):
    key = lax.broadcasted_iota(jnp.int32, scores.shape, 0)
    return jnp.where(key < count, scores, -jnp.inf)


def attention_forward_kernel(
    count, starts_ref, q_ref, k_ref, v_ref, pk_ref, pv_ref, out_ref, lse_ref, vt_ref, pvt_ref, s_ref
):
    length = q_ref.shape[0]
    blocks = length // BLOCK
    vt_ref[...] = v_ref[...].astype(wide).T.astype(low_type)
    pvt_ref[...] = pv_ref[...].astype(wide).T.astype(low_type)
    for i in range(blocks):
        rows = slice(i * BLOCK, (i + 1) * BLOCK)
        start = starts_ref[:, rows]
        query = q_ref[rows, :]
        parts = []
        for h in range(2):
            feats = slice(h * HEAD, (h + 1) * HEAD)
            mine = head_mask(query, h)
            pre = prefix_mask(dot_nt(pk_ref[...], mine), count)
            peak = jnp.max(pre, axis=0, keepdims=True)
            for c in range(i + 1):
                keys = slice(c * BLOCK, (c + 1) * BLOCK)
                s = token_mask(dot_nt(k_ref[keys, :], mine), start, i, c)
                s_ref[h, keys, :] = s
                peak = jnp.maximum(peak, jnp.max(s, axis=0, keepdims=True))
            pre = jnp.exp(pre - peak)
            total = jnp.sum(pre, axis=0, keepdims=True)
            acc = dot(pvt_ref[feats, :], pre.astype(low_type))
            for c in range(i + 1):
                keys = slice(c * BLOCK, (c + 1) * BLOCK)
                p = jnp.exp(s_ref[h, keys, :] - peak)
                total = total + jnp.sum(p, axis=0, keepdims=True)
                acc = acc + dot(vt_ref[feats, keys], p.astype(low_type))
            parts.append(acc / total)
            lse_ref[0, h : h + 1, rows] = peak + jnp.log(total)
        out_ref[rows, :] = jnp.concatenate(parts, axis=0).T.astype(low_type)


def attention_backward_kernel(
    count,
    starts_ref,
    q_ref,
    k_ref,
    v_ref,
    g_ref,
    pk_ref,
    pv_ref,
    lse_ref,
    dq_ref,
    dk_ref,
    dv_ref,
    dpk_ref,
    dpv_ref,
    kt_ref,
    pkt_ref,
    p_ref,
    dp_ref,
    ds_ref,
    dk_acc,
    dv_acc,
):
    length = q_ref.shape[0]
    blocks = length // BLOCK
    kt_ref[...] = k_ref[...].astype(wide).T.astype(low_type)
    pkt_ref[...] = pk_ref[...].astype(wide).T.astype(low_type)
    dk_acc[...] = jnp.zeros_like(dk_acc)
    dv_acc[...] = jnp.zeros_like(dv_acc)
    dpk_ref[...] = jnp.zeros_like(dpk_ref)
    dpv_ref[...] = jnp.zeros_like(dpv_ref)
    for i in range(blocks):
        rows = slice(i * BLOCK, (i + 1) * BLOCK)
        start = starts_ref[:, rows]
        parts = []
        for h in range(2):
            feats = slice(h * HEAD, (h + 1) * HEAD)
            mine = head_mask(q_ref[rows, :], h)
            grad = head_mask(g_ref[rows, :], h)
            lse = lse_ref[0, h : h + 1, rows]
            pre = jnp.exp(prefix_mask(dot_nt(pk_ref[...], mine), count) - lse)
            dpre = dot_nt(pv_ref[...], grad)
            delta = jnp.sum(pre * dpre, axis=0, keepdims=True)
            for c in range(i + 1):
                keys = slice(c * BLOCK, (c + 1) * BLOCK)
                p = jnp.exp(token_mask(dot_nt(k_ref[keys, :], mine), start, i, c) - lse)
                dp = dot_nt(v_ref[keys, :], grad)
                delta = delta + jnp.sum(p * dp, axis=0, keepdims=True)
                p_ref[keys, :] = p
                dp_ref[keys, :] = dp
                dv_acc[keys, :] += dot(p.astype(low_type), grad)
            dpre = (pre * (dpre - delta)).astype(low_type)
            dpv_ref[...] += dot(pre.astype(low_type), grad)
            dpk_ref[...] += dot(dpre, mine)
            acc = dot(pkt_ref[feats, :], dpre)
            for c in range(i + 1):
                keys = slice(c * BLOCK, (c + 1) * BLOCK)
                ds = (p_ref[keys, :] * (dp_ref[keys, :] - delta)).astype(low_type)
                dk_acc[keys, :] += dot(ds, mine)
                acc = acc + dot(kt_ref[feats, keys], ds)
            parts.append(acc)
        dq_ref[rows, :] = (jnp.concatenate(parts, axis=0).T * (HEAD**-0.5)).astype(low_type)
    dk_ref[...] = dk_acc[...].astype(low_type)
    dv_ref[...] = dv_acc[...].astype(low_type)


def attention_forward(starts, qkv, pk, pv, count):
    length, width = qkv.shape[0], qkv.shape[1] // 3
    pairs = width // PAIR
    slab = lambda off: pl.BlockSpec((length, PAIR), lambda p: (0, p + off * pairs))
    small = pl.BlockSpec((PRE, PAIR), lambda p: (0, p))
    return pl.pallas_call(
        functools.partial(attention_forward_kernel, count),
        grid=(pairs,),
        in_specs=[
            pl.BlockSpec((1, length), lambda p: (0, 0)),
            slab(0),
            slab(1),
            slab(2),
            small,
            small,
        ],
        out_specs=[slab(0), pl.BlockSpec((1, 2, length), lambda p: (p, 0, 0))],
        out_shape=[
            jax.ShapeDtypeStruct((length, width), low_type),
            jax.ShapeDtypeStruct((pairs, 2, length), wide),
        ],
        scratch_shapes=[
            pltpu.VMEM((PAIR, length), low_type),
            pltpu.VMEM((PAIR, PRE), low_type),
            pltpu.VMEM((2, length, BLOCK), wide),
        ],
        compiler_params=pltpu.CompilerParams(vmem_limit_bytes=48 << 20),
        cost_estimate=pl.CostEstimate(flops=20_000_000_000, bytes_accessed=10 << 20, transcendentals=0),
    )(starts, qkv, qkv, qkv, pk, pv)


def attention_backward(starts, qkv, grad, pk, pv, lse, count):
    length, width = qkv.shape[0], qkv.shape[1] // 3
    pairs = width // PAIR
    slab = lambda off: pl.BlockSpec((length, PAIR), lambda p: (0, p + off * pairs))
    small = pl.BlockSpec((PRE, PAIR), lambda p: (0, p))
    whole = jax.ShapeDtypeStruct((length, width), low_type)
    return pl.pallas_call(
        functools.partial(attention_backward_kernel, count),
        grid=(pairs,),
        in_specs=[
            pl.BlockSpec((1, length), lambda p: (0, 0)),
            slab(0),
            slab(1),
            slab(2),
            slab(0),
            small,
            small,
            pl.BlockSpec((1, 2, length), lambda p: (p, 0, 0)),
        ],
        out_specs=[slab(0), slab(0), slab(0), small, small],
        out_shape=[whole] * 3 + [jax.ShapeDtypeStruct((PRE, width), wide)] * 2,
        scratch_shapes=[
            pltpu.VMEM((PAIR, length), low_type),
            pltpu.VMEM((PAIR, PRE), low_type),
            pltpu.VMEM((length, BLOCK), wide),
            pltpu.VMEM((length, BLOCK), wide),
            pltpu.VMEM((length, BLOCK), low_type),
            pltpu.VMEM((length, PAIR), wide),
            pltpu.VMEM((length, PAIR), wide),
        ],
        compiler_params=pltpu.CompilerParams(vmem_limit_bytes=48 << 20),
        cost_estimate=pl.CostEstimate(flops=40_000_000_000, bytes_accessed=20 << 20, transcendentals=0),
    )(starts, qkv, qkv, qkv, grad, pk, pv, lse)


def exchange(values):
    return lax.all_to_all(values, "col", split_axis=0, concat_axis=0, tiled=True)


def on_device(
    inputs,
    starts,
    cotangent,
    first_norm_gain,
    shift_one,
    w_qkv,
    b_qkv,
    w_out,
    b_out,
    second_norm_gain,
    shift_two,
    w_fc,
    b_fc,
    w_proj,
    b_proj,
    prefix_table,
    rep_w1,
    rep_b1,
    rep_w2,
    rep_b2,
):
    col_count = lax.axis_size("col")
    row_count, piece_len, model_width = inputs.shape
    assert row_count == col_count
    length = piece_len * col_count
    home = (col_count, piece_len, model_width)

    row_inputs = exchange(inputs).reshape(length, model_width)
    row_starts = exchange(starts).reshape(1, length)
    cotangent, row_inputs = lax.optimization_barrier((cotangent, row_inputs))
    row_cot = exchange(cotangent).reshape(length, model_width)

    pre_act = (
        dense_product("pd,dh->ph", prefix_table.astype(low_type), rep_w1.astype(low_type)) + rep_b1
    )
    hidden = jnp.tanh(pre_act)
    hidden_low = hidden.astype(low_type)
    w2_low = rep_w2.astype(low_type)
    own_cols = (dense_product("ph,hc->pc", hidden_low, w2_low) + rep_b2).astype(low_type)
    prefix_all = lax.all_gather(own_cols, "col", axis=1, tiled=True)
    prefix_rows = prefix_all.shape[0]
    prefix_all = jnp.pad(prefix_all, ((0, PRE - prefix_rows), (0, 0)))
    pk = prefix_all[:, :model_width]
    pv = prefix_all[:, model_width:]

    residual = row_inputs.astype(wide)
    first_gain, second_gain = first_norm_gain.astype(wide), second_norm_gain.astype(wide)
    first_normed, first_standardized, first_inverse = layer_normalize(
        residual, first_gain, shift_one.astype(wide)
    )
    mixed = dot(first_normed.astype(low_type), w_qkv) + b_qkv.astype(wide)
    scale = jnp.where(jnp.arange(3 * model_width) < model_width, HEAD**-0.5, 1.0)
    qkv = (mixed * scale).astype(low_type)
    attended, lse = attention_forward(row_starts, qkv, pk, pv, prefix_rows)
    middle = residual + dot(attended, w_out) + b_out.astype(wide)
    second_normed, second_standardized, second_inverse = layer_normalize(
        middle, second_gain, shift_two.astype(wide)
    )
    upper = dot(second_normed.astype(low_type), w_fc) + b_fc.astype(wide)
    activation, gelu_slope = gelu_parts(upper)
    result = middle + dot(activation.astype(low_type), w_proj) + b_proj.astype(wide)
    output = exchange(result.astype(low_type).reshape(home))

    grad_act = dot_nt(row_cot, w_proj)
    grad_upper = (grad_act * gelu_slope).astype(low_type)
    grad_middle = row_cot.astype(wide) + norm_backward_pass(
        dot_nt(grad_upper, w_fc), second_gain, second_standardized, second_inverse
    )
    grad_attended = dot_nt(grad_middle.astype(low_type), w_out).astype(low_type)
    dq, dk, dv, dpk, dpv = attention_backward(
        row_starts, qkv, grad_attended, pk, pv, lse, prefix_rows
    )
    grad_mixed = jnp.concatenate([dq, dk, dv], axis=-1)
    grad_row = grad_middle + norm_backward_pass(
        dot_nt(grad_mixed, w_qkv), first_gain, first_standardized, first_inverse
    )
    grad_input = exchange(grad_row.astype(low_type).reshape(home))

    prefix_local = jnp.concatenate([dpk[:prefix_rows], dpv[:prefix_rows]], axis=1)
    own_grad = lax.psum_scatter(prefix_local, "col", scatter_dimension=1, tiled=True)
    own_grad = lax.psum(own_grad, "dp")
    own_low = own_grad.astype(low_type)
    grad_w2 = dense_product("ph,pc->hc", hidden_low, own_low)
    grad_b2 = jnp.sum(own_low.astype(wide), axis=0)
    hidden_part = dense_product("pc,hc->ph", own_low, w2_low)
    grad_hidden = lax.psum(hidden_part, "col")
    grad_pre = (grad_hidden * (1.0 - hidden * hidden)).astype(low_type)
    grad_w1 = dense_product("pd,ph->dh", prefix_table.astype(low_type), grad_pre)
    grad_b1 = jnp.sum(grad_pre.astype(wide), axis=0)
    grad_table = dense_product("ph,dh->pd", grad_pre, rep_w1.astype(low_type))
    return (output, grad_input, grad_table, grad_w1, grad_b1, grad_w2, grad_b2)


def solution(mesh):
    rows = P("dp", "col", None)
    return jax.shard_map(
        on_device,
        mesh=mesh,
        in_specs=(rows, P("dp", "col"), rows) + (P(),) * 15 + (P(None, "col"), P("col")),
        out_specs=(rows, rows, P(), P(), P(), P(None, "col"), P("col")),
        check_vma=False,
    )
```

time: 2170 us -> 443 us (0.20)
  waiting for transfers between devices: 1400 us -> 73.7 us
  matrix products: 388 us -> 102 us
  local copies, waits for them, and re-layouts: 170 us -> 8.83 us
  other arithmetic: 102 us -> 16.1 us
  Pallas kernels: 0 us -> 80.9 us
  blocking collectives: 82.3 us -> 113 us
  starting transfers between devices: 0.2 us -> 29.5 us
    reduce_scatter x2 -> x0, waiting for transfers between devices: 1010 us -> none  [the longest x1 542 us: on_device(): lax.psum_scatter(value_terms, 'col', scatter_dimension=1, tiled=True)]
    all_gather x2 -> x0, waiting for transfers between devices: 393 us -> none  [the longest x1 206 us: on_device(): lax.all_gather(value_rows, 'col', axis=1, tiled=True)]
    dot_general x69 -> x6, matrix products: 388 us -> 5.82 us  [dense_product(): jnp.einsum(pattern, left_side, right_side, preferred_element_type=jnp.flo...]
    dot_general x0 -> x7, matrix products: none -> 95.7 us  [the longest x4 48.7 us: dot(): return jnp.dot(a, b, preferred_element_type=wide)]
    pallas_call x0 -> x2, Pallas kernels: none -> 80.9 us  [the longest x1 50.4 us: attention_backward(): pl.pallas_call(functools.partial(attention_backward_kernel, count), grid=...]
    reduce_scatter x1, waiting for transfers between devices: 0.01 us -> 73.7 us  [on_device(): lax.psum_scatter(prefix_local, 'col', scatter_dimension=1, tiled=True)]
    reshape x6 -> x0, local copies, waits for them, and re-layouts: 64.6 us -> none  [the longest x1 32.2 us: on_device(): key_terms = grad_k_all.reshape(row_count, length, model_width)]
    convert_element_type x19 -> x9, other arithmetic: 63.2 us -> 4.65 us  [the longest x1 4.62 us: on_device(): grad_input = exchange(grad_row.astype(low_type).reshape(home))]
  transfers between devices with their start and end apart: 5 -> 6, of which waited for: 4 -> 1; matrix products, arithmetic and copies ran while one was open for 6% -> 27% of each run, Pallas kernels for 0% -> 18%
where the time goes in v1:
time: 443 us; the launch traced here: 438 us
  blocking collectives  113 us (26%)
  matrix products  102 us (23%)
  Pallas kernels  80.9 us (18%)
  waiting for transfers between devices  73.7 us (17%)
  starting transfers between devices  29.5 us (7%)
  other arithmetic  16.1 us (4%)
  between operations  14.9 us (3%)
  local copies, waits for them, and re-layouts  8.83 us (2%)
    reduce_scatter x1, waiting for transfers between devices, on_device(): lax.psum_scatter(prefix_local, 'col', scatter_dimension=1, tiled=True)  73.7 us
    all_gather x1, blocking collectives, on_device(): prefix_all = lax.all_gather(own_cols, 'col', axis=1, tiled=True)  66.7 us
    pallas_call x1, Pallas kernels, attention_backward(): pl.pallas_call(functools.partial(attention_backward_kernel, count), grid=...  50.4 us
    dot_general x4, matrix products, dot(): return jnp.dot(a, b, preferred_element_type=wide)  48.7 us
    dot_general x3, matrix products, dot_nt(): return lax.dot_general(a, b, NT, preferred_element_type=wide)  47 us
    psum x1, blocking collectives, on_device(): grad_hidden = lax.psum(hidden_part, 'col')  35.2 us
    pallas_call x1, Pallas kernels, attention_forward(): pl.pallas_call(functools.partial(attention_forward_kernel, count), grid=(...  30.5 us
    all_to_all x5, starting transfers between devices, exchange(): lax.all_to_all(values, 'col', split_axis=0, concat_axis=0, tiled=True)  29.5 us
  transfers between devices with their start and end apart: 6, of which 1 were waited for; matrix products, arithmetic and copies ran while one was open for 27% of the time, Pallas kernels for 18%

profile of v1, /device:TPU:0, one launch (start us, length us, event | category | flops | bytes accessed | tf_op | source)
XLA Modules:
  0.0 438.0 jit_solution(16598447840550303354)
XLA Ops:
  7.3 7.6 %all-to-all-start = ((bf16[8,128,1024]{2,1,0:T(8,128)(2,1)}), bf16[8,128,1024]{2,1,0:T(8,128)(2,1)}, u32[]{:S(2)}, u32[]{:S(2)}) async-start(bf16[8,128,1024]{2,1,0:T(8,128)(2,1)} %param.20), calls=%async_computation | async-start | bytes 4194304 | tf_op jit(solution)/shard_map/all_to_all | solution.py:246
  16.5 66.7 %all_gather.3 = bf16[10,2048]{1,0:T(8,128)(2,1)S(1)} all-gather(bf16[10,256]{1,0:T(8,128)(2,1)S(1)} %fusion.51), channel_id=1, replica_groups=mesh['dp'=4,'col'=8] {'col'}, dimensions={1}, use_global_device_ids=true | all-gather | bytes 46080 | tf_op jit(solution)/shard_map/all_gather | solution.py:289
  83.2 3.6 all-to-all-start.1
  88.8 2.3 fusion.33
  91.1 12.1 %multiply_convert_fusion.1.q_ref.k_ref.v_ref = bf16[1024,3072]{1,0:T(8,128)(2,1)} fusion(f32[3072]{0:T(1024)S(1)} %fusion.58, f32[3072]{0:T(1024)S(1)} %convert_element_type.92, bf16[1024,3072]{1,0:T(8,128)(2,1)} %param.25, bf16[1024,1024]{1,0:T(8,128)(2,1)} %bitcast, f32[1024]{0:T(1024)S(1)} %convert_element_type.90, f32[1024]{0:T(1024)S(1)} %convert_element_type.89, ...), kind=kOutput, calls=%fused_computation.10 | convolution fusion | flops 6458179584 | bytes 14721024 | tf_op jit(solution)/shard_map/dot_general | solution.py:55
  103.2 6.2 %all-to-all-start.3 = ((bf16[8,128,1024]{2,1,0:T(8,128)(2,1)}), bf16[8,128,1024]{2,1,0:T(8,128)(2,1)}, u32[]{:S(2)}, u32[]{:S(2)}) async-start(bf16[8,128,1024]{2,1,0:T(8,128)(2,1)} %param.22), calls=%async_computation.3 | async-start | bytes 4194304 | tf_op jit(solution)/shard_map/all_to_all | solution.py:246
  109.4 30.5 %shard_map.243 = (bf16[1024,1024]{1,0:T(8,128)(2,1)S(1)}, f32[8,2,1024]{2,1,0:T(2,128)S(1)}) custom-call(s32[1,1024]{1,0:T(1,128)S(1)} %bitcast.27, bf16[1024,3072]{1,0:T(8,128)(2,1)} %multiply_convert_fusion.1.q_ref.k_ref.v_ref, bf16[1024,3072]{1,0:T(8,128)(2,1)} %multiply_convert_fusion.1.q_ref.k_ref.v_ref, ...), custom_call_target="tpu_custom_call" | custom-call | flops 20000000000 | bytes 10485760 | tf_op jit(solution)/shard_map/pallas_call | solution.py:184
  140.0 4.1 fusion.76
  144.7 16.8 %fusion.35 = f32[1024,4096]{1,0:T(8,128)} fusion(bf16[1024,4096]{1,0:T(8,128)(2,1)} %param.31, f32[1024,1024]{1,0:T(8,128)S(1)} %get-tuple-element.48, f32[1024]{0:T(1024)S(1)} %convert_element_type.101, f32[1024]{0:T(1024)S(1)} %convert_element_type.100, f32[1024]{0:T(1024)S(1)} %add_rsqrt_fusion, f32[1024]{0:T(1024)S(1)} %broadcast_multiply_fusion.4), kind=kOutput, calls=%fused_computation.50 | convolution fusion | flops 8595177472 | bytes 29376512 | tf_op jit(solution)/shard_map/dot_general | solution.py:55
  161.5 15.7 %add_convert_fusion = bf16[1024,1024]{1,0:T(8,128)(2,1)} fusion(f32[1024,1024]{1,0:T(8,128)S(1)} %get-tuple-element.48, f32[1024]{0:T(1024)S(1)} %convert_element_type.105, bf16[4096,1024]{1,0:T(8,128)(2,1)S(1)} %bitcast.32, f32[1024,4096]{1,0:T(8,128)} %fusion.35, f32[4096]{0:T(1024)S(1)} %convert_element_type.103), kind=kOutput, calls=%fused_computation.44 | convolution fusion | flops 8635023360 | bytes 31477760 | tf_op jit(solution)/shard_map/dot_general | solution.py:55
  177.2 6.0 %all-to-all-start.2 = ((bf16[8,128,1024]{2,1,0:T(8,128)(2,1)}), bf16[8,128,1024]{2,1,0:T(8,128)(2,1)}, u32[]{:S(2)}, u32[]{:S(2)}) async-start(bf16[8,128,1024]{2,1,0:T(8,128)(2,1)} %bitcast.30), calls=%async_computation.2 | async-start | bytes 4194304 | tf_op jit(solution)/shard_map/all_to_all | solution.py:246
  183.2 31.3 %multiply_reduce_fusion.3 = (f32[1024]{0:T(1024)S(1)}, f32[1024]{0:T(1024)S(1)}, f32[1024,1024]{1,0:T(8,128)}) fusion(f32[1024]{0:T(1024)S(1)} %convert_element_type.100, f32[1024]{0:T(1024)S(1)} %add_rsqrt_fusion, f32[1024,1024]{1,0:T(8,128)} %copy-done.1, f32[1024]{0:T(1024)S(1)} %broadcast_multiply_fusion.4, bf16[1024,4096]{1,0:T(8,128)(2,1)} %param.31, ...), kind=kOutput, calls=%fused_computation.49 | convolution fusion | flops 17270046720 | bytes 44077056 | tf_op jit(solution)/shard_map/dot_general | solution.py:51
  214.5 4.8 %multiply_add_fusion.1 = f32[1024,1024]{1,0:T(8,128)S(1)} fusion(f32[1024,1024]{1,0:T(8,128)} %get-tuple-element.49, f32[1024,1024]{1,0:T(8,128)} %copy-done.1, f32[1024]{0:T(1024)S(1)} %get-tuple-element.51, f32[1024]{0:T(1024)S(1)} %get-tuple-element.52, f32[1024]{0:T(1024)S(1)} %convert_element_type.100, f32[1024]{0:T(1024)S(1)} %add_rsqrt_fusion, ...), kind=kLoop, calls=%fused_computation.42 | loop fusion | flops 9437184 | bytes 14700544 | tf_op jit(solution)/shard_map/add | solution.py:315
  219.2 3.7 fusion.47.g_ref
  222.9 50.4 %shard_map.244 = (bf16[1024,1024]{1,0:T(8,128)(2,1)S(1)}, bf16[1024,1024]{1,0:T(8,128)(2,1)S(1)}, bf16[1024,1024]{1,0:T(8,128)(2,1)}, f32[16,1024]{1,0:T(8,128)S(1)}, f32[16,1024]{1,0:T(8,128)S(1)}) custom-call(s32[1,1024]{1,0:T(1,128)S(1)} %bitcast.28, bf16[1024,3072]{1,0:T(8,128)(2,1)} %multiply_convert_fusion.1.q_ref.k_ref.v_ref, ...), custom_call_target="tpu_custom_call" | custom-call | flops 40000000000 | bytes 20971520 | tf_op jit(solution)/shard_map/pallas_call | solution.py:216
  273.3 12.1 %multiply_reduce_fusion.2 = (f32[1024]{0:T(1024)S(1)}, f32[1024]{0:T(1024)S(1)}, f32[1024,1024]{1,0:T(8,128)}) fusion(f32[1024]{0:T(1024)S(1)} %copy-done.11, f32[1024]{0:T(1024)S(1)} %copy-done.13, f32[1024]{0:T(1024)S(1)} %copy-done.9, bf16[1024,1024]{1,0:T(8,128)(2,1)} %bitcast, bf16[1024,3072]{1,0:T(8,128)(2,1)} %param.25, ...), kind=kOutput, calls=%fused_computation.48 | convolution fusion | flops 6468663296 | bytes 18894848 | tf_op jit(solution)/shard_map/dot_general | solution.py:51
  285.4 4.6 %fusion.32 = bf16[1024,1024]{1,0:T(8,128)(2,1)} fusion(f32[1024,1024]{1,0:T(8,128)S(1)} %multiply_add_fusion.1, bf16[1024,1024]{1,0:T(8,128)(2,1)} %bitcast, f32[1024,1024]{1,0:T(8,128)} %get-tuple-element.50, f32[1024]{0:T(1024)S(1)} %broadcast_multiply_fusion, f32[1024]{0:T(1024)S(1)} %broadcast_multiply_fusion.1, f32[1024]{0:T(1024)S(1)} %copy-done.11, ...), kind=kLoop, calls=%fused_computation.39 | loop fusion | flops 10485760 | bytes 12603392 | tf_op jit(solution)/shard_map/convert_element_type | solution.py:326
  290.0 6.1 %all-to-all-start.4 = ((bf16[8,128,1024]{2,1,0:T(8,128)(2,1)}), bf16[8,128,1024]{2,1,0:T(8,128)(2,1)}, u32[]{:S(2)}, u32[]{:S(2)}) async-start(bf16[8,128,1024]{2,1,0:T(8,128)(2,1)} %bitcast.29), calls=%async_computation.4 | async-start | bytes 4194304 | tf_op jit(solution)/shard_map/all_to_all | solution.py:246
  296.9 73.7 %reduce-scatter.2.cloned.1.call-done = f32[10,256]{1,0:T(8,128)} async-done(((f32[10,2048]{1,0:T(8,128)}), f32[10,256]{1,0:T(8,128)}) %reduce-scatter.2.cloned.1.call-update) | async-done | bytes 10256 | tf_op jit(solution)/shard_map/reduce_scatter | solution.py:329
  370.5 10.7 %psum.14 = bf16[10,256]{1,0:T(8,128)(2,1)S(1)} all-reduce(f32[10,256]{1,0:T(8,128)} %reduce-scatter.2.cloned.1.call-done), channel_id=1, replica_groups=mesh['dp'=4,'col'=8] {'dp'}, use_global_device_ids=true, to_apply=%region_9.10 | all-reduce | flops 2560 | bytes 15360 | tf_op jit(solution)/shard_map/psum | solution.py:330
  382.4 35.2 %psum.15 = f32[10,512]{1,0:T(8,128)S(1)} all-reduce(f32[10,512]{1,0:T(8,128)S(1)} %fusion.55), channel_id=1, replica_groups=mesh['dp'=4,'col'=8] {'col'}, use_global_device_ids=true, to_apply=%region_10.11 | all-reduce | flops 5120 | bytes 40960 | tf_op jit(solution)/shard_map/psum | solution.py:335
  419.5 2.5 copy.28
  424.6 3.1 copy.31
  427.6 3.1 copy.32
  (88 shorter events, 10.4 us)
Async XLA Ops:
  7.2 132.8 %copy-start = (bf16[1024,1024]{1,0:T(8,128)(2,1)S(1)}, bf16[1024,1024]{1,0:T(8,128)(2,1)}, u32[]{:S(2)}) copy-start(bf16[1024,1024]{1,0:T(8,128)(2,1)} %param.27) | copy-start | bytes 6291460
  7.3 7.8 %copy-start.14 = (bf16[4096]{0:T(1024)(128)(2,1)S(1)}, bf16[4096]{0:T(1024)(128)(2,1)}, u32[]{:S(2)}) copy-start(bf16[4096]{0:T(1024)(128)(2,1)} %param.32) | copy-start | bytes 24580
  7.3 7.8 %copy-start.2 = (f32[512,512]{1,0:T(8,128)S(1)}, f32[512,512]{1,0:T(8,128)}, u32[]{:S(2)}) copy-start(f32[512,512]{1,0:T(8,128)} %param.36) | copy-start | bytes 3145732
  7.3 7.8 %copy-start.6 = (f32[10,512]{1,0:T(8,128)S(1)}, f32[10,512]{1,0:T(8,128)}, u32[]{:S(2)}) copy-start(f32[10,512]{1,0:T(8,128)} %param.35) | copy-start | bytes 61444
  7.3 7.8 %copy-start.16 = (f32[512]{0:T(512)S(1)}, f32[512]{0:T(512)}, u32[]{:S(2)}) copy-start(f32[512]{0:T(512)} %param.37) | copy-start | bytes 6148
  7.3 8.0 %copy-start.23 = (f32[256]{0:T(256)S(1)}, f32[256]{0:T(256)}, u32[]{:S(2)}) copy-start(f32[256]{0:T(256)} %param.39) | copy-start | bytes 3076
  7.3 75.9 %all-to-all-start = ((bf16[8,128,1024]{2,1,0:T(8,128)(2,1)}), bf16[8,128,1024]{2,1,0:T(8,128)(2,1)}, u32[]{:S(2)}, u32[]{:S(2)}) async-start(bf16[8,128,1024]{2,1,0:T(8,128)(2,1)} %param.20), calls=%async_computation | async-start | bytes 4194304 | tf_op jit(solution)/shard_map/all_to_all | solution.py:246
  14.9 88.3 %copy-start.10 = (f32[1024]{0:T(1024)}, f32[1024]{0:T(1024)S(1)}, u32[]{:S(2)}) copy-start(f32[1024]{0:T(1024)S(1)} %convert_element_type.89) | copy-start | bytes 12292
  15.3 67.9 %copy-start.4 = (f32[10,512]{1,0:T(8,128)}, f32[10,512]{1,0:T(8,128)S(1)}, u32[]{:S(2)}) copy-start(f32[10,512]{1,0:T(8,128)S(1)} %fusion.50) | copy-start | bytes 61444
  83.2 20.0 %all-to-all-start.1 = ((s32[8,1,128]{2,1,0:T(1,128)}), s32[8,1,128]{2,1,0:T(1,128)S(1)}, u32[]{:S(2)}, u32[]{:S(2)}) async-start(s32[8,1,128]{2,1,0:T(1,128)} %bitcast.1), calls=%async_computation.1 | async-start | bytes 8192 | tf_op jit(solution)/shard_map/all_to_all | solution.py:246
  91.1 12.1 %copy-start.12 = (f32[1024]{0:T(1024)}, f32[1024]{0:T(1024)S(1)}, u32[]{:S(2)}) copy-start(f32[1024]{0:T(1024)S(1)} %add_rsqrt_fusion.1) | copy-start | bytes 12292
  103.2 74.0 %all-to-all-start.3 = ((bf16[8,128,1024]{2,1,0:T(8,128)(2,1)}), bf16[8,128,1024]{2,1,0:T(8,128)(2,1)}, u32[]{:S(2)}, u32[]{:S(2)}) async-start(bf16[8,128,1024]{2,1,0:T(8,128)(2,1)} %param.22), calls=%async_computation.3 | async-start | bytes 4194304 | tf_op jit(solution)/shard_map/all_to_all | solution.py:246
  144.1 17.4 %copy-start.1 = (f32[1024,1024]{1,0:T(8,128)}, f32[1024,1024]{1,0:T(8,128)S(1)}, u32[]{:S(2)}) copy-start(f32[1024,1024]{1,0:T(8,128)S(1)} %get-tuple-element.48) | copy-start | bytes 12582916
  144.1 17.4 %slice-start = ((s8[8388608]{0:T(1024)(128)(4,1)}), s8[4194304]{0:T(1024)(128)(4,1)S(1)}, s32[]{:S(2)}) async-start(s8[8388608]{0:T(1024)(128)(4,1)} %bitcast.31), calls=%async_computation.7 | async-start | bytes 8388608
  144.7 16.8 %slice-start.1 = ((s8[8388608]{0:T(1024)(128)(4,1)}), s8[4194304]{0:T(1024)(128)(4,1)S(1)}, s32[]{:S(2)}) async-start(s8[8388608]{0:T(1024)(128)(4,1)} %bitcast.31), calls=%async_computation.8 | async-start | bytes 8388608
  177.2 112.8 %all-to-all-start.2 = ((bf16[8,128,1024]{2,1,0:T(8,128)(2,1)}), bf16[8,128,1024]{2,1,0:T(8,128)(2,1)}, u32[]{:S(2)}, u32[]{:S(2)}) async-start(bf16[8,128,1024]{2,1,0:T(8,128)(2,1)} %bitcast.30), calls=%async_computation.2 | async-start | bytes 4194304 | tf_op jit(solution)/shard_map/all_to_all | solution.py:246
  222.9 50.4 %copy-start.9 = (f32[1024]{0:T(1024)S(1)}, f32[1024]{0:T(1024)}, u32[]{:S(2)}) copy-start(f32[1024]{0:T(1024)} %copy-done.8) | copy-start | bytes 12292
  222.9 50.4 %copy-start.11 = (f32[1024]{0:T(1024)S(1)}, f32[1024]{0:T(1024)}, u32[]{:S(2)}) copy-start(f32[1024]{0:T(1024)} %copy-done.10) | copy-start | bytes 12292
  222.9 50.4 %copy-start.13 = (f32[1024]{0:T(1024)S(1)}, f32[1024]{0:T(1024)}, u32[]{:S(2)}) copy-start(f32[1024]{0:T(1024)} %copy-done.12) | copy-start | bytes 12292
  290.0 127.6 %copy-start.5 = (f32[10,512]{1,0:T(8,128)S(1)}, f32[10,512]{1,0:T(8,128)}, u32[]{:S(2)}) copy-start(f32[10,512]{1,0:T(8,128)} %copy-done.4) | copy-start | bytes 61444
  290.0 128.2 %copy-start.7 = (f32[10,512]{1,0:T(8,128)S(1)}, f32[10,512]{1,0:T(8,128)}, u32[]{:S(2)}) copy-start(f32[10,512]{1,0:T(8,128)} %param.35) | copy-start | bytes 61444
  290.0 133.7 %copy-start.3 = (f32[512,512]{1,0:T(8,128)S(1)}, f32[512,512]{1,0:T(8,128)}, u32[]{:S(2)}) copy-start(f32[512,512]{1,0:T(8,128)} %param.36) | copy-start | bytes 3145732
  290.0 134.5 %all-to-all-start.4 = ((bf16[8,128,1024]{2,1,0:T(8,128)(2,1)}), bf16[8,128,1024]{2,1,0:T(8,128)(2,1)}, u32[]{:S(2)}, u32[]{:S(2)}) async-start(bf16[8,128,1024]{2,1,0:T(8,128)(2,1)} %bitcast.29), calls=%async_computation.4 | async-start | bytes 4194304 | tf_op jit(solution)/shard_map/all_to_all | solution.py:246
  296.1 74.4 %reduce-scatter.2.cloned.1.call-start = ((), (), s32[]{:S(2)}) async-start(), calls=%async_computation.6 | async-start | bytes 147456 | tf_op jit(solution)/shard_map/reduce_scatter | solution.py:329
  (8 other events, 56.4 us)
Sparse Core Ops, SparseCore 0:
  300.9 69.6 reduce-scatter.1

commit v2 on v1

--- a/solution.py
+++ b/solution.py
@@ -19,13 +19,16 @@
 low_type = jnp.bfloat16
 wide = jnp.float32
 NT = (((1,), (1,)), ((), ()))
-
-
-def layer_normalize(values, norm_gain, norm_shift):
+TN = (((0,), (0,)), ((), ()))
+MESH = pl.DeviceIdType.MESH
+ANY = pl.BlockSpec(memory_space=pl.ANY)
+VM = pl.BlockSpec(memory_space=pltpu.VMEM)
+
+
+def standardize(values):
     center = values - jnp.mean(values, axis=-1, keepdims=True)
     inverse = lax.rsqrt(jnp.mean(center * center, axis=-1, keepdims=True) + epsilon)
-    normed = center * inverse
-    return (normed * norm_gain + norm_shift, normed, inverse)
+    return center * inverse, inverse
 
 
 def norm_backward_pass(gradient, norm_gain, normed, inverse):
@@ -34,17 +37,15 @@
     return inverse * (centered - normed * jnp.mean(scaled * normed, axis=-1, keepdims=True))
 
 
-def gelu_parts(upper_rows):
-    tangent = jnp.tanh(gelu_coef * (upper_rows + cubic_coef * upper_rows * upper_rows * upper_rows))
-    gelu_value = 0.5 * upper_rows * (1.0 + tangent)
-    gelu_slope = 0.5 * (1.0 + tangent) + 0.5 * upper_rows * (
-        1.0 - tangent * tangent
-    ) * gelu_coef * (1.0 + 3.0 * cubic_coef * upper_rows * upper_rows)
-    return (gelu_value, gelu_slope)
-
-
-def dense_product(pattern, left_side, right_side):
-    return jnp.einsum(pattern, left_side, right_side, preferred_element_type=jnp.float32)
+def gelu_parts(upper):
+    square = upper * upper
+    tangent = jnp.tanh(upper * (gelu_coef + (gelu_coef * cubic_coef) * square))
+    half = 0.5 * upper
+    share = 0.5 + 0.5 * tangent
+    slope = share + half * (1.0 - tangent * tangent) * (
+        gelu_coef + (3.0 * gelu_coef * cubic_coef) * square
+    )
+    return upper * share, slope
 
 
 def dot_nt(a, b):
@@ -242,6 +243,583 @@
     )(starts, qkv, qkv, qkv, grad, pk, pv, lse)
 
 
+def greet(peers):
+    barrier = pltpu.get_barrier_semaphore()
+    for peer in peers:
+        pl.semaphore_signal(barrier, inc=1, device_id=peer, device_id_type=MESH)
+    pl.semaphore_wait(barrier, len(peers))
+
+
+def far_first(count):
+    return sorted(range(1, count), key=lambda d: (abs(2 * d - count), d))
+
+
+def arrive_kernel(
+    n,
+    x_hbm,
+    starts_hbm,
+    w_hbm,
+    table_ref,
+    w1_ref,
+    b1_ref,
+    w2_ref,
+    b2_ref,
+    gain_ref,
+    shift_ref,
+    bias_ref,
+    x_out,
+    starts_out,
+    qkv_out,
+    pk_out,
+    pv_out,
+    hidden_out,
+    x_rows,
+    h_rows,
+    qkv_rows,
+    w_rows,
+    own_pre,
+    pre_slots,
+    x_send,
+    x_recv,
+    s_send,
+    s_recv,
+    p_send,
+    p_recv,
+    local_sem,
+    store_sem,
+):
+    me = lax.axis_index("col")
+    piece, width = x_hbm.shape[1], x_hbm.shape[2]
+    greet([{"col": lax.rem(me + d, n)} for d in range(1, n)])
+    mine = pl.ds(pl.multiple_of(me * piece, piece), piece)
+    sends = []
+    for d in far_first(n):
+        peer = {"col": lax.rem(me + d, n)}
+        copy = pltpu.make_async_remote_copy(
+            src_ref=x_hbm.at[lax.rem(me + d, n)],
+            dst_ref=x_rows.at[mine, :],
+            send_sem=x_send.at[d],
+            recv_sem=x_recv.at[d],
+            device_id=peer,
+            device_id_type=MESH,
+        )
+        copy.start()
+        small = pltpu.make_async_remote_copy(
+            src_ref=starts_hbm.at[lax.rem(me + d, n)],
+            dst_ref=starts_out.at[me],
+            send_sem=s_send.at[d],
+            recv_sem=s_recv.at[d],
+            device_id=peer,
+            device_id_type=MESH,
+        )
+        small.start()
+        sends += [(d, copy), (d, small)]
+    own_x = pltpu.make_async_copy(x_hbm.at[me], x_rows.at[mine, :], local_sem.at[0])
+    own_x.start()
+    own_starts = pltpu.make_async_copy(starts_hbm.at[me], starts_out.at[me], local_sem.at[1])
+    own_starts.start()
+    load_w = pltpu.make_async_copy(w_hbm, w_rows, local_sem.at[2])
+    load_w.start()
+
+    hidden = jnp.tanh(dot(table_ref[...].astype(low_type), w1_ref[...].astype(low_type)) + b1_ref[...])
+    rows = hidden.shape[0]
+    hidden_out[...] = jnp.concatenate([hidden, jnp.zeros((PRE - rows, hidden.shape[1]), wide)], 0)
+    own = dot(hidden.astype(low_type), w2_ref[...].astype(low_type)) + b2_ref[...]
+    own = jnp.concatenate([own, jnp.zeros((PRE - rows, own.shape[1]), wide)], 0).astype(low_type)
+    own_pre[...] = own
+    pre_slots[me] = own
+    for d in far_first(n):
+        copy = pltpu.make_async_remote_copy(
+            src_ref=own_pre,
+            dst_ref=pre_slots.at[me],
+            send_sem=p_send.at[d],
+            recv_sem=p_recv.at[d],
+            device_id={"col": lax.rem(me + d, n)},
+            device_id_type=MESH,
+        )
+        copy.start()
+        sends.append((d, copy))
+
+    gain, shift = gain_ref[...].astype(wide), shift_ref[...].astype(wide)
+    group = max(1, BLOCK // piece)
+    order = [0] + far_first(n)[::-1]
+    own_x.wait()
+    load_w.wait()
+    stores = []
+    for g in range(0, n, group):
+        spots = []
+        for j, d in enumerate(order[g : g + group]):
+            source = lax.rem(me + n - d, n)
+            spot = pl.ds(pl.multiple_of(source * piece, piece), piece)
+            spots.append(spot)
+            if d:
+                pltpu.make_async_remote_copy(
+                    src_ref=x_hbm.at[source],
+                    dst_ref=x_rows.at[spot, :],
+                    send_sem=x_send.at[d],
+                    recv_sem=x_recv.at[d],
+                    device_id={"col": source},
+                    device_id_type=MESH,
+                ).wait_recv()
+            store = pltpu.make_async_copy(x_rows.at[spot, :], x_out.at[spot, :], store_sem.at[0, d])
+            store.start()
+            stores.append(store)
+            normed, _ = standardize(x_rows[spot, :].astype(wide))
+            h_rows[j * piece : (j + 1) * piece, :] = (normed * gain + shift).astype(low_type)
+        for c in range(0, 3 * width, width // 2):
+            cols = slice(c, c + width // 2)
+            part = dot(h_rows[...], w_rows[:, cols]) + bias_ref[:, cols].astype(wide)
+            if c < width:
+                part = part * (HEAD**-0.5)
+            part = part.astype(low_type)
+            for j, spot in enumerate(spots):
+                qkv_rows[spot, cols] = part[j * piece : (j + 1) * piece, :]
+        for j, d in enumerate(order[g : g + group]):
+            store = pltpu.make_async_copy(
+                qkv_rows.at[spots[j], :], qkv_out.at[spots[j], :], store_sem.at[1, d]
+            )
+            store.start()
+            stores.append(store)
+    for d in far_first(n):
+        source = lax.rem(me + n - d, n)
+        for src, dst, send, recv in (
+            (starts_hbm.at[source], starts_out.at[source], s_send, s_recv),
+            (own_pre, pre_slots.at[source], p_send, p_recv),
+        ):
+            pltpu.make_async_remote_copy(
+                src_ref=src,
+                dst_ref=dst,
+                send_sem=send.at[d],
+                recv_sem=recv.at[d],
+                device_id={"col": source},
+                device_id_type=MESH,
+            ).wait_recv()
+    part_width = own.shape[1]
+    for j in range(n):
+        lo = j * part_width
+        if lo < width:
+            pk_out[:, lo : lo + part_width] = pre_slots[j]
+        else:
+            pv_out[:, lo - width : lo - width + part_width] = pre_slots[j]
+    for _, copy in sends:
+        copy.wait_send()
+    own_starts.wait()
+    for store in stores:
+        store.wait()
+
+
+def arrive(inputs, starts, w_qkv, table, w1, b1, w2, b2, gain, shift, bias):
+    n, piece, width = inputs.shape
+    length = n * piece
+    part_width = w2.shape[1]
+    dma = pltpu.SemaphoreType.DMA
+    return pl.pallas_call(
+        functools.partial(arrive_kernel, n),
+        in_specs=[ANY, ANY, ANY] + [VM] * 8,
+        out_specs=[ANY, ANY, ANY, VM, VM, VM],
+        out_shape=[
+            jax.ShapeDtypeStruct((length, width), low_type),
+            jax.ShapeDtypeStruct((n, 1, piece), jnp.int32),
+            jax.ShapeDtypeStruct((length, 3 * width), low_type),
+            jax.ShapeDtypeStruct((PRE, width), low_type),
+            jax.ShapeDtypeStruct((PRE, width), low_type),
+            jax.ShapeDtypeStruct((PRE, w1.shape[1]), wide),
+        ],
+        scratch_shapes=[
+            pltpu.VMEM((length, width), low_type),
+            pltpu.VMEM((BLOCK, width), low_type),
+            pltpu.VMEM((length, 3 * width), low_type),
+            pltpu.VMEM(w_qkv.shape, low_type),
+            pltpu.VMEM((PRE, part_width), low_type),
+            pltpu.VMEM((n, PRE, part_width), low_type),
+            dma((n,)),
+            dma((n,)),
+            dma((n,)),
+            dma((n,)),
+            dma((n,)),
+            dma((n,)),
+            dma((3,)),
+            dma((2, n)),
+        ],
+        compiler_params=pltpu.CompilerParams(
+            collective_id=0, has_side_effects=True, vmem_limit_bytes=56 << 20
+        ),
+    )(inputs, starts, w_qkv, table, w1, b1, w2, b2, gain, shift, bias)
+
+
+def leave_kernel(
+    n,
+    n_dp,
+    dq_hbm,
+    dk_hbm,
+    dv_hbm,
+    w_hbm,
+    x_hbm,
+    mid_hbm,
+    gain_ref,
+    dpk_ref,
+    dpv_ref,
+    hidden_ref,
+    table_ref,
+    w1_ref,
+    w2_ref,
+    grad_out,
+    table_out,
+    gw1_out,
+    gb1_out,
+    gw2_out,
+    gb2_out,
+    g_rows,
+    w_rows,
+    x_rows,
+    mid_rows,
+    staged,
+    local_pre,
+    col_slots,
+    dp_own,
+    dp_slots,
+    hid_own,
+    hid_slots,
+    send_sem,
+    recv_sem,
+    c_send,
+    c_recv,
+    d_send,
+    d_recv,
+    h_send,
+    h_recv,
+    load_sem,
+    local_sem,
+):
+    me = lax.axis_index("col")
+    me_dp = lax.axis_index("dp")
+    piece, width = grad_out.shape[1], grad_out.shape[2]
+    length = n * piece
+    loads = []
+    for j, (src, dst) in enumerate(
+        (
+            (dq_hbm, g_rows.at[:, 0:width]),
+            (dk_hbm, g_rows.at[:, width : 2 * width]),
+            (dv_hbm, g_rows.at[:, 2 * width : 3 * width]),
+            (w_hbm, w_rows),
+            (x_hbm, x_rows),
+            (mid_hbm, mid_rows),
+        )
+    ):
+        load = pltpu.make_async_copy(src, dst, load_sem.at[j])
+        load.start()
+        loads.append(load)
+    greet(
+        [{"col": lax.rem(me + d, n)} for d in range(1, n)]
+        + [{"dp": lax.rem(me_dp + d, n_dp)} for d in range(1, n_dp)]
+    )
+    part_width = w2_ref.shape[1]
+    local_pre[:, 0:width] = dpk_ref[...]
+    local_pre[:, width : 2 * width] = dpv_ref[...]
+    sends = []
+
+    def push(src, dst, send, recv, d, axis, me_at, count):
+        copy = pltpu.make_async_remote_copy(
+            src_ref=src,
+            dst_ref=dst,
+            send_sem=send.at[d],
+            recv_sem=recv.at[d],
+            device_id={axis: lax.rem(me_at + d, count)},
+            device_id_type=MESH,
+        )
+        copy.start()
+        sends.append(copy)
+
+    def catch(src, dst, send, recv, d, axis, source):
+        pltpu.make_async_remote_copy(
+            src_ref=src,
+            dst_ref=dst,
+            send_sem=send.at[d],
+            recv_sem=recv.at[d],
+            device_id={axis: source},
+            device_id_type=MESH,
+        ).wait_recv()
+
+    def slice_of(owner):
+        return local_pre.at[:, pl.ds(pl.multiple_of(owner * part_width, part_width), part_width)]
+
+    for d in far_first(n):
+        push(slice_of(lax.rem(me + d, n)), col_slots.at[me], c_send, c_recv, d, "col", me, n)
+    col_slots[me] = local_pre[:, pl.ds(pl.multiple_of(me * part_width, part_width), part_width)]
+    for load in loads:
+        load.wait()
+    gain = gain_ref[...].astype(wide)
+    hidden = hidden_ref[...]
+    hidden_low = hidden.astype(low_type)
+    w2_low = w2_ref[...].astype(low_type)
+
+    def gradient_group(g, order):
+        group = order[g : g + max(1, BLOCK // piece)]
+        spots = [lax.rem(me + d, n) for d in group]
+        parts = [
+            g_rows[pl.ds(pl.multiple_of(spot * piece, piece), piece), :] for spot in spots
+        ]
+        block = jnp.concatenate(parts, axis=0)
+        back = dot_nt(block, w_rows[...])
+        for j, (d, spot) in enumerate(zip(group, spots)):
+            rows = pl.ds(pl.multiple_of(spot * piece, piece), piece)
+            normed, inverse = standardize(x_rows[rows, :].astype(wide))
+            total = mid_rows[rows, :] + norm_backward_pass(
+                back[j * piece : (j + 1) * piece, :], gain, normed, inverse
+            )
+            staged[d] = total.astype(low_type)
+            if d:
+                push(staged.at[d], grad_out.at[me], send_sem, recv_sem, d, "col", me, n)
+            else:
+                pltpu.make_async_copy(staged.at[0], grad_out.at[me], local_sem.at[0]).start()
+
+    order = far_first(n) + [0]
+    step = max(1, BLOCK // piece)
+    groups = list(range(0, n, step))
+    gradient_group(groups[0], order)
+    for d in range(1, n):
+        source = lax.rem(me + n - d, n)
+        catch(slice_of(source), col_slots.at[source], c_send, c_recv, d, "col", source)
+    total = col_slots[0]
+    for j in range(1, n):
+        total = total + col_slots[j]
+    dp_own[...] = total
+    dp_slots[me_dp] = total
+    for d in range(1, n_dp):
+        push(dp_own, dp_slots.at[me_dp], d_send, d_recv, d, "dp", me_dp, n_dp)
+    gradient_group(groups[1], order)
+    for d in range(1, n_dp):
+        source = lax.rem(me_dp + n_dp - d, n_dp)
+        catch(dp_own, dp_slots.at[source], d_send, d_recv, d, "dp", source)
+    total = dp_slots[0]
+    for j in range(1, n_dp):
+        total = total + dp_slots[j]
+    own_low = total.astype(low_type)
+    part = dot_nt(own_low, w2_low)
+    hid_own[...] = part
+    hid_slots[me] = part
+    for d in far_first(n):
+        push(hid_own, hid_slots.at[me], h_send, h_recv, d, "col", me, n)
+    for g in groups[2:]:
+        gradient_group(g, order)
+    gw2_out[...] = lax.dot_general(hidden_low, own_low, TN, preferred_element_type=wide)
+    gb2_out[...] = jnp.sum(own_low.astype(wide), axis=0, keepdims=True)
+    for d in range(1, n):
+        source = lax.rem(me + n - d, n)
+        catch(hid_own, hid_slots.at[source], h_send, h_recv, d, "col", source)
+    total = hid_slots[0]
+    for j in range(1, n):
+        total = total + hid_slots[j]
+    grad_pre = (total * (1.0 - hidden * hidden)).astype(low_type)
+    rows = table_ref.shape[0]
+    table = jnp.concatenate(
+        [table_ref[...], jnp.zeros((PRE - rows, table_ref.shape[1]), wide)], 0
+    ).astype(low_type)
+    gw1_out[...] = lax.dot_general(table, grad_pre, TN, preferred_element_type=wide)
+    gb1_out[...] = jnp.sum(grad_pre.astype(wide), axis=0, keepdims=True)
+    table_out[...] = dot_nt(grad_pre, w1_ref[...].astype(low_type))[:rows, :]
+    for d in range(1, n):
+        source = lax.rem(me + n - d, n)
+        catch(staged.at[d], grad_out.at[source], send_sem, recv_sem, d, "col", source)
+    pltpu.make_async_copy(staged.at[0], grad_out.at[me], local_sem.at[0]).wait()
+    for copy in sends:
+        copy.wait_send()
+
+
+def leave(n, n_dp, dq, dk, dv, w_qkv, rows, mid, gain, dpk, dpv, hidden, table, w1, w2):
+    length, width = rows.shape
+    piece = length // n
+    part_width = w2.shape[1]
+    dma = pltpu.SemaphoreType.DMA
+    shape = jax.ShapeDtypeStruct
+    return pl.pallas_call(
+        functools.partial(leave_kernel, n, n_dp),
+        in_specs=[ANY] * 6 + [VM] * 7,
+        out_specs=[ANY] + [VM] * 5,
+        out_shape=[
+            shape((n, piece, width), low_type),
+            shape(table.shape, wide),
+            shape(w1.shape, wide),
+            shape((1, w1.shape[1]), wide),
+            shape(w2.shape, wide),
+            shape((1, part_width), wide),
+        ],
+        scratch_shapes=[
+            pltpu.VMEM((length, 3 * width), low_type),
+            pltpu.VMEM(w_qkv.shape, low_type),
+            pltpu.VMEM((length, width), low_type),
+            pltpu.VMEM((length, width), wide),
+            pltpu.VMEM((n, piece, width), low_type),
+            pltpu.VMEM((PRE, 2 * width), wide),
+            pltpu.VMEM((n, PRE, part_width), wide),
+            pltpu.VMEM((PRE, part_width), wide),
+            pltpu.VMEM((n_dp, PRE, part_width), wide),
+            pltpu.VMEM((PRE, w1.shape[1]), wide),
+            pltpu.VMEM((n, PRE, w1.shape[1]), wide),
+            dma((n,)),
+            dma((n,)),
+            dma((n,)),
+            dma((n,)),
+            dma((n_dp,)),
+            dma((n_dp,)),
+            dma((n,)),
+            dma((n,)),
+            dma((6,)),
+            dma((1,)),
+        ],
+        compiler_params=pltpu.CompilerParams(
+            collective_id=1, has_side_effects=True, vmem_limit_bytes=56 << 20
+        ),
+    )(dq, dk, dv, w_qkv, rows, mid, gain, dpk, dpv, hidden, table, w1, w2)
+
+
+def feed_forward_kernel(
+    att_ref,
+    x_ref,
+    w_out_ref,
+    b_out_ref,
+    gain_ref,
+    shift_ref,
+    w_fc_ref,
+    b_fc_ref,
+    w_proj_ref,
+    b_proj_ref,
+    out_ref,
+    mid_ref,
+    slope_ref,
+    h_ref,
+    acc_ref,
+):
+    step = pl.program_id(0)
+    chunks = [slice(r, r + 2 * BLOCK) for r in range(0, att_ref.shape[0], 2 * BLOCK)]
+
+    @pl.when(step == 0)
+    def _():
+        for r in chunks:
+            mid = x_ref[r, :].astype(wide) + dot(att_ref[r, :], w_out_ref[...])
+            mid = mid + b_out_ref[...].astype(wide)
+            mid_ref[r, :] = mid
+            normed, _ = standardize(mid)
+            h = normed * gain_ref[...].astype(wide) + shift_ref[...].astype(wide)
+            h_ref[r, :] = h.astype(low_type)
+            acc_ref[r, :] = mid + b_proj_ref[...].astype(wide)
+
+    for r in chunks:
+        upper = dot(h_ref[r, :], w_fc_ref[...]) + b_fc_ref[...].astype(wide)
+        value, slope = gelu_parts(upper)
+        slope_ref[r, :] = slope.astype(low_type)
+        acc_ref[r, :] += dot(value.astype(low_type), w_proj_ref[...])
+
+    @pl.when(step == pl.num_programs(0) - 1)
+    def _():
+        out_ref[...] = acc_ref[...].astype(low_type)
+
+
+def feed_forward(att, rows, w_out, b_out, gain, shift, w_fc, b_fc, w_proj, b_proj):
+    length, width = rows.shape
+    inner = w_fc.shape[1]
+    tile = min(1024, inner)
+    full = lambda a: pl.BlockSpec(a.shape, lambda t: (0,) * a.ndim)
+    whole = pl.BlockSpec((length, width), lambda t: (0, 0))
+    return pl.pallas_call(
+        feed_forward_kernel,
+        grid=(inner // tile,),
+        in_specs=[
+            full(att),
+            full(rows),
+            full(w_out),
+            full(b_out),
+            full(gain),
+            full(shift),
+            pl.BlockSpec((width, tile), lambda t: (0, t)),
+            pl.BlockSpec((1, tile), lambda t: (0, t)),
+            pl.BlockSpec((tile, width), lambda t: (t, 0)),
+            full(b_proj),
+        ],
+        out_specs=[whole, whole, pl.BlockSpec((length, tile), lambda t: (0, t))],
+        out_shape=[
+            jax.ShapeDtypeStruct((length, width), low_type),
+            jax.ShapeDtypeStruct((length, width), wide),
+            jax.ShapeDtypeStruct((length, inner), low_type),
+        ],
+        scratch_shapes=[pltpu.VMEM((length, width), low_type), pltpu.VMEM((length, width), wide)],
+        compiler_params=pltpu.CompilerParams(vmem_limit_bytes=56 << 20),
+        cost_estimate=pl.CostEstimate(
+            flops=2 * length * width * (width + 2 * inner),
+            bytes_accessed=40 << 20,
+            transcendentals=length * inner,
+        ),
+    )(att, rows, w_out, b_out, gain, shift, w_fc, b_fc, w_proj, b_proj)
+
+
+def feed_backward_kernel(
+    cot_ref,
+    slope_ref,
+    w_proj_ref,
+    w_fc_ref,
+    mid_ref,
+    gain_ref,
+    w_out_ref,
+    grad_mid_ref,
+    grad_att_ref,
+    acc_ref,
+):
+    step = pl.program_id(0)
+    chunks = [slice(r, r + 2 * BLOCK) for r in range(0, cot_ref.shape[0], 2 * BLOCK)]
+
+    @pl.when(step == 0)
+    def _():
+        acc_ref[...] = jnp.zeros_like(acc_ref)
+
+    for r in chunks:
+        grad_act = dot_nt(cot_ref[r, :], w_proj_ref[...])
+        grad_upper = (grad_act * slope_ref[r, :].astype(wide)).astype(low_type)
+        acc_ref[r, :] += dot_nt(grad_upper, w_fc_ref[...])
+
+    @pl.when(step == pl.num_programs(0) - 1)
+    def _():
+        for r in chunks:
+            normed, inverse = standardize(mid_ref[r, :])
+            grad_mid = cot_ref[r, :].astype(wide) + norm_backward_pass(
+                acc_ref[r, :], gain_ref[...].astype(wide), normed, inverse
+            )
+            grad_mid_ref[r, :] = grad_mid
+            grad_att_ref[r, :] = dot_nt(grad_mid.astype(low_type), w_out_ref[...]).astype(low_type)
+
+
+def feed_backward(cot, slope, w_proj, w_fc, mid, gain, w_out):
+    length, width = cot.shape
+    inner = w_fc.shape[1]
+    tile = min(1024, inner)
+    full = lambda a: pl.BlockSpec(a.shape, lambda t: (0,) * a.ndim)
+    whole = pl.BlockSpec((length, width), lambda t: (0, 0))
+    return pl.pallas_call(
+        feed_backward_kernel,
+        grid=(inner // tile,),
+        in_specs=[
+            full(cot),
+            pl.BlockSpec((length, tile), lambda t: (0, t)),
+            pl.BlockSpec((tile, width), lambda t: (t, 0)),
+            pl.BlockSpec((width, tile), lambda t: (0, t)),
+            full(mid),
+            full(gain),
+            full(w_out),
+        ],
+        out_specs=[whole, whole],
+        out_shape=[
+            jax.ShapeDtypeStruct((length, width), wide),
+            jax.ShapeDtypeStruct((length, width), low_type),
+        ],
+        scratch_shapes=[pltpu.VMEM((length, width), wide)],
+        compiler_params=pltpu.CompilerParams(vmem_limit_bytes=56 << 20),
+        cost_estimate=pl.CostEstimate(
+            flops=2 * length * width * (width + 2 * inner),
+            bytes_accessed=40 << 20,
+            transcendentals=0,
+        ),
+    )(cot, slope, w_proj, w_fc, mid, gain, w_out)
+
+
 def exchange(values):
     return lax.all_to_all(values, "col", split_axis=0, concat_axis=0, tiled=True)
 
@@ -268,76 +846,79 @@
     rep_w2,
     rep_b2,
 ):
-    col_count = lax.axis_size("col")
+    col_count, dp_count = lax.axis_size("col"), lax.axis_size("dp")
     row_count, piece_len, model_width = inputs.shape
     assert row_count == col_count
     length = piece_len * col_count
     home = (col_count, piece_len, model_width)
-
-    row_inputs = exchange(inputs).reshape(length, model_width)
-    row_starts = exchange(starts).reshape(1, length)
-    cotangent, row_inputs = lax.optimization_barrier((cotangent, row_inputs))
+    prefix_rows = prefix_table.shape[0]
+    flat = lambda v: v.reshape(1, -1)
+
+    rows, row_starts, qkv, pk, pv, hidden = arrive(
+        inputs,
+        starts.reshape(col_count, 1, piece_len),
+        w_qkv,
+        prefix_table,
+        rep_w1,
+        flat(rep_b1),
+        rep_w2,
+        flat(rep_b2),
+        flat(first_norm_gain),
+        flat(shift_one),
+        flat(b_qkv),
+    )
+    cotangent, qkv = lax.optimization_barrier((cotangent, qkv))
     row_cot = exchange(cotangent).reshape(length, model_width)
-
-    pre_act = (
-        dense_product("pd,dh->ph", prefix_table.astype(low_type), rep_w1.astype(low_type)) + rep_b1
+    row_starts = row_starts.reshape(1, length)
+
+    attended, lse = attention_forward(row_starts, qkv, pk, pv, prefix_rows)
+    result, middle, slope = feed_forward(
+        attended,
+        rows,
+        w_out,
+        flat(b_out),
+        flat(second_norm_gain),
+        flat(shift_two),
+        w_fc,
+        flat(b_fc),
+        w_proj,
+        flat(b_proj),
     )
-    hidden = jnp.tanh(pre_act)
-    hidden_low = hidden.astype(low_type)
-    w2_low = rep_w2.astype(low_type)
-    own_cols = (dense_product("ph,hc->pc", hidden_low, w2_low) + rep_b2).astype(low_type)
-    prefix_all = lax.all_gather(own_cols, "col", axis=1, tiled=True)
-    prefix_rows = prefix_all.shape[0]
-    prefix_all = jnp.pad(prefix_all, ((0, PRE - prefix_rows), (0, 0)))
-    pk = prefix_all[:, :model_width]
-    pv = prefix_all[:, model_width:]
-
-    residual = row_inputs.astype(wide)
-    first_gain, second_gain = first_norm_gain.astype(wide), second_norm_gain.astype(wide)
-    first_normed, first_standardized, first_inverse = layer_normalize(
-        residual, first_gain, shift_one.astype(wide)
+    output = exchange(result.reshape(home))
+
+    grad_middle, grad_attended = feed_backward(
+        row_cot, slope, w_proj, w_fc, middle, flat(second_norm_gain), w_out
     )
-    mixed = dot(first_normed.astype(low_type), w_qkv) + b_qkv.astype(wide)
-    scale = jnp.where(jnp.arange(3 * model_width) < model_width, HEAD**-0.5, 1.0)
-    qkv = (mixed * scale).astype(low_type)
-    attended, lse = attention_forward(row_starts, qkv, pk, pv, prefix_rows)
-    middle = residual + dot(attended, w_out) + b_out.astype(wide)
-    second_normed, second_standardized, second_inverse = layer_normalize(
-        middle, second_gain, shift_two.astype(wide)
-    )
-    upper = dot(second_normed.astype(low_type), w_fc) + b_fc.astype(wide)
-    activation, gelu_slope = gelu_parts(upper)
-    result = middle + dot(activation.astype(low_type), w_proj) + b_proj.astype(wide)
-    output = exchange(result.astype(low_type).reshape(home))
-
-    grad_act = dot_nt(row_cot, w_proj)
-    grad_upper = (grad_act * gelu_slope).astype(low_type)
-    grad_middle = row_cot.astype(wide) + norm_backward_pass(
-        dot_nt(grad_upper, w_fc), second_gain, second_standardized, second_inverse
-    )
-    grad_attended = dot_nt(grad_middle.astype(low_type), w_out).astype(low_type)
     dq, dk, dv, dpk, dpv = attention_backward(
         row_starts, qkv, grad_attended, pk, pv, lse, prefix_rows
     )
-    grad_mixed = jnp.concatenate([dq, dk, dv], axis=-1)
-    grad_row = grad_middle + norm_backward_pass(
-        dot_nt(grad_mixed, w_qkv), first_gain, first_standardized, first_inverse
+    dq, output = lax.optimization_barrier((dq, output))
+    grad_input, grad_table, grad_w1, grad_b1, grad_w2, grad_b2 = leave(
+        col_count,
+        dp_count,
+        dq,
+        dk,
+        dv,
+        w_qkv,
+        rows,
+        grad_middle,
+        flat(first_norm_gain),
+        dpk,
+        dpv,
+        hidden,
+        prefix_table,
+        rep_w1,
+        rep_w2,
     )
-    grad_input = exchange(grad_row.astype(low_type).reshape(home))
-
-    prefix_local = jnp.concatenate([dpk[:prefix_rows], dpv[:prefix_rows]], axis=1)
-    own_grad = lax.psum_scatter(prefix_local, "col", scatter_dimension=1, tiled=True)
-    own_grad = lax.psum(own_grad, "dp")
-    own_low = own_grad.astype(low_type)
-    grad_w2 = dense_product("ph,pc->hc", hidden_low, own_low)
-    grad_b2 = jnp.sum(own_low.astype(wide), axis=0)
-    hidden_part = dense_product("pc,hc->ph", own_low, w2_low)
-    grad_hidden = lax.psum(hidden_part, "col")
-    grad_pre = (grad_hidden * (1.0 - hidden * hidden)).astype(low_type)
-    grad_w1 = dense_product("pd,ph->dh", prefix_table.astype(low_type), grad_pre)
-    grad_b1 = jnp.sum(grad_pre.astype(wide), axis=0)
-    grad_table = dense_product("ph,dh->pd", grad_pre, rep_w1.astype(low_type))
-    return (output, grad_input, grad_table, grad_w1, grad_b1, grad_w2, grad_b2)
+    return (
+        output,
+        grad_input,
+        grad_table,
+        grad_w1,
+        grad_b1.reshape(-1),
+        grad_w2,
+        grad_b2.reshape(-1),
+    )
 
 
 def solution(mesh):

time: 443 us -> 309 us (0.70)
  the two profiles are of different devices: /device:TPU:0 before, /device:TPU:19 now
where the time goes in v2:
time: 309 us; the launch traced here: 303 us
  Pallas kernels  270 us (87%)
  local copies, waits for them, and re-layouts  19.4 us (6%)
  starting transfers between devices  12.6 us (4%)
    pallas_call x1, Pallas kernels, leave(): pl.pallas_call(functools.partial(leave_kernel, n, n_dp), in_specs=[ANY] *...  64.8 us
    pallas_call x1, Pallas kernels, arrive(): pl.pallas_call(functools.partial(arrive_kernel, n), in_specs=[ANY, ANY, A...  60 us
    pallas_call x1, Pallas kernels, attention_backward(): pl.pallas_call(functools.partial(attention_backward_kernel, count), grid=...  50.3 us
    pallas_call x1, Pallas kernels, feed_forward(): pl.pallas_call(feed_forward_kernel, grid=(inner // tile,), in_specs=[full...  33.2 us
    pallas_call x1, Pallas kernels, feed_backward(): pl.pallas_call(feed_backward_kernel, grid=(inner // tile,), in_specs=[ful...  31.2 us
    pallas_call x1, Pallas kernels, attention_forward(): pl.pallas_call(functools.partial(attention_forward_kernel, count), grid=(...  30.5 us
    all_to_all x2, starting transfers between devices, exchange(): lax.all_to_all(values, 'col', split_axis=0, concat_axis=0, tiled=True)  12.6 us
    unnamed x45, local copies, waits for them, and re-layouts  12.5 us
  transfers between devices with their start and end apart: 2, of which 0 were waited for; matrix products, arithmetic and copies ran while one was open for 1% of the time, Pallas kernels for 48%

profile of v2, /device:TPU:19, one launch (start us, length us, event | category | flops | bytes accessed | tf_op | source)
XLA Modules:
  0.0 303.3 jit_solution(11248454612297683485)
XLA Ops:
  0.6 1.3 reshape.67.gain_ref
  1.9 1.3 reshape.68.shift_ref
  3.2 1.3 reshape.69.bias_ref
  4.5 60.0 %shard_map.243 = (bf16[1024,1024]{1,0:T(8,128)(2,1)}, s32[8,1,128]{2,1,0:T(1,128)}, bf16[1024,3072]{1,0:T(8,128)(2,1)}, bf16[16,1024]{1,0:T(8,128)(2,1)}, bf16[16,1024]{1,0:T(8,128)(2,1)}, /*index=5*/f32[16,512]{1,0:T(8,128)}) custom-call(bf16[8,128,1024]{2,1,0:T(8,128)(2,1)} %x_hbm.1, s32[8,1,128]{2,1,0:T(1,128)} %bitcast.11, bf16[1024,3072]{1,0:T(8,128)(2,1)} %w_hbm.3, ...), custom_call_target="tpu_custom_call" | custom-call | tf_op jit(solution)/shard_map/pallas_call | solution.py:416
  64.6 6.9 %all-to-all-start = ((bf16[8,128,1024]{2,1,0:T(8,128)(2,1)}), bf16[8,128,1024]{2,1,0:T(8,128)(2,1)}, u32[]{:S(2)}, u32[]{:S(2)}) async-start(bf16[8,128,1024]{2,1,0:T(8,128)(2,1)} %param.22), calls=%async_computation | async-start | bytes 4194304 | tf_op jit(solution)/shard_map/all_to_all | solution.py:824
  71.5 0.6 reshape.73.gain_ref
  73.9 0.6 reshape.75.b_fc_ref
  74.5 30.5 %shard_map.244 = (bf16[1024,1024]{1,0:T(8,128)(2,1)S(1)}, f32[8,2,1024]{2,1,0:T(2,128)S(1)}) custom-call(s32[1,1024]{1,0:T(1,128)S(1)} %bitcast.8, bf16[1024,3072]{1,0:T(8,128)(2,1)} %get-tuple-element.37.q_ref.k_ref.v_ref, bf16[1024,3072]{1,0:T(8,128)(2,1)} %get-tuple-element.37.q_ref.k_ref.v_ref, bf16[1024,3072]{1,0:T(8,128)(2,1)} %get-tuple-element.37.q_ref.k_ref.v_ref, ...), custom_call_target="tpu_custom_call" | custom-call | flops 20000000000 | bytes 10485760 | tf_op jit(solution)/shard_map/pallas_call | solution.py:185
  105.1 1.3 copy-done.7
  106.4 33.2 %shard_map.245 = (bf16[1024,1024]{1,0:T(8,128)(2,1)}, f32[1024,1024]{1,0:T(8,128)}, bf16[1024,4096]{1,0:T(8,128)(2,1)}) custom-call(bf16[1024,1024]{1,0:T(8,128)(2,1)} %copy-done.7, bf16[1024,1024]{1,0:T(8,128)(2,1)} %get-tuple-element.42.x_ref.x_hbm, bf16[1024,1024]{1,0:T(8,128)(2,1)} %w_out_ref.3, bf16[1,1024]{1,0:T(2,128)(2,1)} %reshape.72.b_out_ref, ...), custom_call_target="tpu_custom_call" | custom-call | flops 19327352832 | bytes 41943040 | tf_op jit(solution)/shard_map/pallas_call | solution.py:724
  139.7 5.7 %all-to-all-start.1 = ((bf16[8,128,1024]{2,1,0:T(8,128)(2,1)}), bf16[8,128,1024]{2,1,0:T(8,128)(2,1)S(1)}, u32[]{:S(2)}, u32[]{:S(2)}) async-start(bf16[8,128,1024]{2,1,0:T(8,128)(2,1)} %bitcast.10), calls=%async_computation.1 | async-start | bytes 4194304 | tf_op jit(solution)/shard_map/all_to_all | solution.py:824
  145.3 31.2 %shard_map.246 = (f32[1024,1024]{1,0:T(8,128)}, bf16[1024,1024]{1,0:T(8,128)(2,1)}) custom-call(bf16[1024,1024]{1,0:T(8,128)(2,1)} %bitcast.4.cot_ref, bf16[1024,4096]{1,0:T(8,128)(2,1)} %get-tuple-element.43.slope_ref, bf16[4096,1024]{1,0:T(8,128)(2,1)} %w_proj_ref.3, bf16[1024,4096]{1,0:T(8,128)(2,1)} %w_fc_ref.3, f32[1024,1024]{1,0:T(8,128)} %get-tuple-element.44.mid_ref, ...), custom_call_target="tpu_custom_call" | custom-call | flops 19327352832 | bytes 41943040 | tf_op jit(solution)/shard_map/pallas_call | solution.py:796
  176.5 50.3 %shard_map.247 = (bf16[1024,1024]{1,0:T(8,128)(2,1)S(1)}, bf16[1024,1024]{1,0:T(8,128)(2,1)S(1)}, bf16[1024,1024]{1,0:T(8,128)(2,1)}, f32[16,1024]{1,0:T(8,128)S(1)}, f32[16,1024]{1,0:T(8,128)S(1)}) custom-call(s32[1,1024]{1,0:T(1,128)S(1)} %bitcast.9, bf16[1024,3072]{1,0:T(8,128)(2,1)} %get-tuple-element.37.q_ref.k_ref.v_ref, ...), custom_call_target="tpu_custom_call" | custom-call | flops 40000000000 | bytes 20971520 | tf_op jit(solution)/shard_map/pallas_call | solution.py:217
  226.9 1.3 copy-done
  228.2 1.3 copy-done.1
  229.5 0.6 copy-done.2
  230.2 0.6 copy-done.3
  230.8 64.8 %shard_map.248 = (bf16[8,128,1024]{2,1,0:T(8,128)(2,1)}, f32[10,512]{1,0:T(8,128)}, f32[512,512]{1,0:T(8,128)}, f32[1,512]{1,0:T(1,128)}, f32[512,256]{1,0:T(8,128)}, /*index=5*/f32[1,256]{1,0:T(1,128)}) custom-call(bf16[1024,1024]{1,0:T(8,128)(2,1)} %copy-done, bf16[1024,1024]{1,0:T(8,128)(2,1)} %copy-done.1, bf16[1024,1024]{1,0:T(8,128)(2,1)} %get-tuple-element.52.dv_hbm, ...), custom_call_target="tpu_custom_call" | custom-call | tf_op jit(solution)/shard_map/pallas_call | solution.py:635
  295.6 1.3 copy.34
  296.9 1.0 copy-done.8
  297.9 1.3 copy.35
  299.2 0.6 copy.36
  299.9 1.0 copy.37
  301.5 0.8 copy.39
  (39 shorter events, 3.1 us)
Async XLA Ops:
  64.5 7.0 %copy-start.13 = (bf16[1024]{0:T(1024)(128)(2,1)S(1)}, bf16[1024]{0:T(1024)(128)(2,1)}, u32[]{:S(2)}) copy-start(bf16[1024]{0:T(1024)(128)(2,1)} %param.29) | copy-start | bytes 6148
  64.5 7.6 %copy-start.14 = (bf16[1024]{0:T(1024)(128)(2,1)S(1)}, bf16[1024]{0:T(1024)(128)(2,1)}, u32[]{:S(2)}) copy-start(bf16[1024]{0:T(1024)(128)(2,1)} %param.28) | copy-start | bytes 6148
  64.5 8.2 %copy-start.15 = (bf16[1024]{0:T(1024)(128)(2,1)S(1)}, bf16[1024]{0:T(1024)(128)(2,1)}, u32[]{:S(2)}) copy-start(bf16[1024]{0:T(1024)(128)(2,1)} %param.30) | copy-start | bytes 6148
  64.5 8.8 %copy-start.16 = (bf16[1024]{0:T(1024)(128)(2,1)S(1)}, bf16[1024]{0:T(1024)(128)(2,1)}, u32[]{:S(2)}) copy-start(bf16[1024]{0:T(1024)(128)(2,1)} %param.34) | copy-start | bytes 6148
  64.5 9.4 %copy-start.12 = (bf16[4096]{0:T(1024)(128)(2,1)S(1)}, bf16[4096]{0:T(1024)(128)(2,1)}, u32[]{:S(2)}) copy-start(bf16[4096]{0:T(1024)(128)(2,1)} %param.32) | copy-start | bytes 24580
  64.6 10.0 %copy-start.4 = (bf16[16,1024]{1,0:T(8,128)(2,1)S(1)}, bf16[16,1024]{1,0:T(8,128)(2,1)}, u32[]{:S(2)}) copy-start(bf16[16,1024]{1,0:T(8,128)(2,1)} %get-tuple-element.39.pk_ref) | copy-start | bytes 98308
  64.6 10.0 %copy-start.5 = (bf16[16,1024]{1,0:T(8,128)(2,1)S(1)}, bf16[16,1024]{1,0:T(8,128)(2,1)}, u32[]{:S(2)}) copy-start(bf16[16,1024]{1,0:T(8,128)(2,1)} %get-tuple-element.40.pv_ref) | copy-start | bytes 98308
  64.6 10.0 %copy-start.6 = (s32[8,1,128]{2,1,0:T(1,128)S(1)}, s32[8,1,128]{2,1,0:T(1,128)}, u32[]{:S(2)}) copy-start(s32[8,1,128]{2,1,0:T(1,128)} %get-tuple-element.35) | copy-start | bytes 12292
  64.6 75.1 %all-to-all-start = ((bf16[8,128,1024]{2,1,0:T(8,128)(2,1)}), bf16[8,128,1024]{2,1,0:T(8,128)(2,1)}, u32[]{:S(2)}, u32[]{:S(2)}) async-start(bf16[8,128,1024]{2,1,0:T(8,128)(2,1)} %param.22), calls=%async_computation | async-start | bytes 4194304 | tf_op jit(solution)/shard_map/all_to_all | solution.py:824
  105.1 1.3 copy-start.7
  139.7 91.1 %all-to-all-start.1 = ((bf16[8,128,1024]{2,1,0:T(8,128)(2,1)}), bf16[8,128,1024]{2,1,0:T(8,128)(2,1)S(1)}, u32[]{:S(2)}, u32[]{:S(2)}) async-start(bf16[8,128,1024]{2,1,0:T(8,128)(2,1)} %bitcast.10), calls=%async_computation.1 | async-start | bytes 4194304 | tf_op jit(solution)/shard_map/all_to_all | solution.py:824
  226.9 1.3 copy-start
  228.2 1.3 copy-start.1
  229.5 0.6 copy-start.2
  230.2 0.6 copy-start.3
  295.6 2.3 copy-start.8
  297.9 1.3 copy-start.11
  297.9 2.0 copy-start.9
  299.2 1.6 copy-start.17
  299.2 2.2 copy-start.10
  299.2 3.0 copy-start.18
